TPU v7x, 256 devices: a whole 4x4x8 slice. The times are simulated.
256 devices in a mesh: gx: 16 (over z_hi, y), gy: 8 (over x, core), sa: 2 (over z_lo).
Axes of the slice: x: 4, y: 4, z: 8 (z_hi: 4, z_lo: 2; z = z_hi * 2 + z_lo), core: 2. Of those that a mesh axis runs over, the one named last changes fastest.
Arguments:
- moments: bfloat16 [2, 16, 16, 128, 1024], P('sa', None, None, 'gx', 'gy'), may hold values from -6 to 6
- speed_x: bfloat16 [2, 16, 128, 1024], P('sa', None, 'gx', 'gy'), may hold values from 0.19921875 to 1.1953125
- flag_x: int32 [2, 16, 128, 1024], P('sa', None, 'gx', 'gy'), may hold values 0 or 1
- speed_y: bfloat16 [2, 16, 128, 1024], P('sa', None, 'gx', 'gy'), may hold values from 0.19921875 to 1.1953125
- flag_y: int32 [2, 16, 128, 1024], P('sa', None, 'gx', 'gy'), may hold values 0 or 1
- w_in: float32 [16, 64], replicated, may hold values from -1.5 to 1.5
- b_in: float32 [64], replicated, may hold values from -3 to 3
- w_mid: float32 [64, 64], replicated, may hold values from -0.75 to 0.75
- b_mid: float32 [64], replicated, may hold values from -3 to 3
- w_out: float32 [64, 16], replicated, may hold values from -0.75 to 0.75
- b_out: float32 [16], replicated, may hold values from -4 to 4
- final_cot: float32 [2, 16, 16, 128, 1024], P('sa', None, None, 'gx', 'gy'), may hold values from -24 to 31
Outputs:
- grad_moments: float32 [2, 16, 16, 128, 1024], P('sa', None, None, 'gx', 'gy')
- grad_w_in: float32 [16, 64], replicated
- grad_b_in: float32 [64], replicated
- grad_w_mid: float32 [64, 64], replicated
- grad_b_mid: float32 [64], replicated
- grad_w_out: float32 [64, 16], replicated
- grad_b_out: float32 [16], replicated
All inputs are finite; a program needn't handle non-finite values. No bound on the sum of `flag_x` or of `flag_y` on one device may be relied on, other than what follows from the above.
Results may differ from a plain program's by a relative error of at most 0.0025.
Values may be sent and summed in bfloat16 or wider, within the bound.
No kernel may reach another device: no remote copies, remote signals or barrier semaphores. Data moves between devices by JAX's collectives and lax.ppermute only.
A program may use at most 128 MiB of HBM per device.

v0:
```python
import jax
import jax.numpy as jnp
from jax import lax
from jax.experimental import pallas as pl
from jax.experimental.pallas import tpu as pltpu
from jax.sharding import Mesh, PartitionSpec as P

f32 = jnp.float32
bf16 = jnp.bfloat16

NN = (((1,), (0,)), ((), ()))
NT = (((1,), (1,)), ((), ()))
TN = (((0,), (0,)), ((), ()))


def mm(a, b, dims=NN):
    return lax.dot_general(a, b, dims, preferred_element_type=f32)


def split(value):
    high = value.astype(bf16)
    return high, (value - high.astype(f32)).astype(bf16)


def iota(shape, dim):
    return lax.broadcasted_iota(jnp.int32, shape, dim)


def edge_picker(rows, length):
    row, lane = iota((2 * rows, length), 0), iota((2 * rows, length), 1)
    spot = jnp.where(row < rows, row * 128 + 127, (row - rows) * 128)
    return jnp.where(lane == spot, 1.0, 0.0).astype(bf16)


def pack_kernel(
    mom, cot, sx, fx, sy, fy, s0, v0, x_up, x_down, y_up, y_down, mom_wide, edge_wide
):
    mom_wide[...] = mom[...].astype(f32)
    edge_wide[0:128, :] = sx[...].astype(f32)
    edge_wide[128:256, :] = fx[...].astype(f32)

    def plane(z, carry):
        rows = pl.ds(pl.multiple_of(z * 16, 16), 16)
        rows_cot = pl.ds(pl.multiple_of(256 + z * 16, 16), 16)
        for x in range(8):
            tile = mom_wide[pl.ds(z * 8 + x, 16, stride=128), :].astype(bf16)
            other = cot[pl.ds(z * 8 + x, 16, stride=128), :]
            s0[rows, x * 128 : x * 128 + 128] = tile
            v0[rows, x * 128 : x * 128 + 128] = other
            if x == 7:
                x_up[rows, :] = tile
                x_up[rows_cot, :] = other.astype(bf16)
            if x == 0:
                x_down[rows, :] = tile
                x_down[rows_cot, :] = other.astype(bf16)
        return carry

    lax.fori_loop(0, 16, plane, 0)
    x_up[512:528, :] = edge_wide[pl.ds(7, 16, stride=8), :].astype(bf16)
    x_up[528:544, :] = edge_wide[pl.ds(128 + 7, 16, stride=8), :].astype(bf16)
    pick = edge_picker(8, 1024)
    ends = mm(pick, s0[...], NT)
    ends_cot = mm(pick, v0[...].astype(bf16), NT)
    y_up[:, 0:256] = ends[0:8]
    y_up[:, 256:512] = ends_cot[0:8]
    y_down[:, 0:256] = ends[8:16]
    y_down[:, 256:512] = ends_cot[8:16]
    last = jnp.where(iota((8, 128), 1) == 127, 1.0, 0.0).astype(bf16)
    y_up[:, 512:640] = mm(last, sy[...], NT)
    y_up[:, 640:768] = mm(last, fy[...].astype(f32).astype(bf16), NT)


def stacked(matrix):
    high, low = split(matrix)
    high, low = high.astype(f32), low.astype(f32)
    return jnp.concatenate([high, high, low], 0)


def bias_rows(bias):
    first = bias.astype(bf16).astype(f32)
    rest = bias - first
    second = rest.astype(bf16).astype(f32)
    third = rest - second
    row = iota((16, bias.shape[1]), 0)
    return jnp.where(row == 0, first, jnp.where(row == 1, second, jnp.where(row == 2, third, 0.0)))


def turned(matrix):
    return matrix.T.astype(bf16)


def three(pair):
    return [pair[0], pair[1], pair[0]]


def main_kernel(
    s0, v0, sx, fx, sy, fy, x_prev, x_next, y_prev, y_next,
    w_in, b_in, w_mid, b_mid, w_out, b_out,
    part, edge_coefs, x_up, x_down, y_up, y_down, sums,
    coefs, moment_ends, cot_ends, v1_held, total,
):
    flag = fx[...].astype(f32) * 0.25
    speed = sx[...].astype(f32)
    push_x, pull_x = speed * flag, speed * (0.25 - flag)
    flag = fy[...].astype(f32) * 0.25
    speed = sy[...].astype(f32)
    push_y, pull_y = speed * flag, speed * (0.25 - flag)
    row, lane = iota((128, 128), 0), iota((128, 128), 1)
    speed_prev = x_prev[512:528, :].astype(f32)
    flag_prev = x_prev[528:544, :].astype(f32) * 0.25
    wide = lambda item: jnp.broadcast_to(item[:, None, :], (16, 8, 128)).reshape(128, 128)
    first_row = lax.rem(row, 8) == 0
    pushed_x = jnp.where(first_row, wide(speed_prev * flag_prev), pltpu.roll(push_x, 1, 0))
    pulled_x = jnp.where(first_row, wide(speed_prev * (0.25 - flag_prev)), pltpu.roll(pull_x, 1, 0))
    place = jnp.where((iota((8, 128), 0) == 0) & (iota((8, 128), 1) == 0), 1.0, 0.0).astype(bf16)
    speed_prev = mm(y_prev[:, 512:640].astype(bf16), place, TN)
    flag_prev = mm(y_prev[:, 640:768].astype(bf16), place, TN) * 0.25
    pushed_y = jnp.where(lane == 0, speed_prev * flag_prev, pltpu.roll(push_y, 1, 1))
    pulled_y = jnp.where(lane == 0, speed_prev * (0.25 - flag_prev), pltpu.roll(pull_y, 1, 1))
    keep = push_x + pulled_x + push_y + pulled_y
    for index, item in enumerate(
        (keep, pull_x, pushed_x, pull_y, pushed_y, push_x, pulled_x, push_y, pulled_y)
    ):
        coefs[index * 128 : index * 128 + 128, :] = item
    for index, item in enumerate((push_x, pulled_x, push_y, pulled_y)):
        edge_coefs[index * 128 : index * 128 + 128, :] = item

    pick = edge_picker(8, 1024)
    ends = jnp.concatenate([y_next[...], y_prev[:, 0:512]], 0).astype(bf16)
    moment_ends[...] = mm(ends[:, 0:256], pick, TN)
    cot_ends[...] = mm(ends[:, 256:512], pick, TN)

    w_in_, w_mid_, w_out_ = w_in[...], w_mid[...], w_out[...]
    in_high, in_low = split(w_in_)
    in_high, in_low = in_high.astype(f32), in_low.astype(f32)
    go_in0 = turned(jnp.concatenate([in_high, in_low, bias_rows(b_in[...])], 0))
    go_in1 = turned(jnp.concatenate([in_high, in_high, in_low, bias_rows(b_in[...])], 0))
    go_mid = turned(jnp.concatenate([stacked(w_mid_), bias_rows(b_mid[...])], 0))
    go_out = turned(jnp.concatenate([stacked(w_out_ * 0.25), bias_rows(b_out[...] * 0.25)], 0))
    back_out = turned(stacked((w_out_ * 0.25).T))
    back_mid = turned(stacked(w_mid_.T))
    back_in = turned(stacked(w_in_.T))
    ones = jnp.full((16, 1024), 1.0, bf16)
    zeros = jnp.zeros((16, 1024), bf16)
    total[...] = jnp.zeros_like(total)
    end_lane = iota((16, 128), 1)

    def stencil(tiles, before, after, ends, z, first):
        around = [before] + tiles + [after]
        results = []
        for x in range(8):
            c = [
                coefs[pl.ds(k * 128 + z * 8 + x, 1), :] for k in (0, first, first + 1, first + 2, first + 3)
            ]
            here = around[x + 1]
            value = c[0] * here
            if around[x + 2] is not None:
                value = value - c[1] * around[x + 2]
            if around[x] is not None:
                value = value - c[2] * around[x]
            right, left = pltpu.roll(here, 127, 1), pltpu.roll(here, 1, 1)
            if ends is None:
                end = 0.0
            else:
                end = ends[x]
            right = jnp.where(end_lane == 127, end, right)
            left = jnp.where(end_lane == 0, end, left)
            value = value - c[3] * right - c[4] * left
            results.append(value)
        return results

    def tiles_of(value):
        return [value[:, x * 128 : x * 128 + 128] for x in range(8)]

    def join(tiles):
        return jnp.concatenate(tiles, 1)

    def cat(items):
        return jnp.concatenate(items, 0)

    def layers(lead, inputs):
        one = jnp.tanh(mm(lead, cat(inputs)))
        one_pair = split(one)
        two = jnp.tanh(mm(go_mid, cat(three(one_pair) + [ones])))
        return one, one_pair, two, split(two)

    def backward(state_pair, one, one_pair, two, two_pair, adjoint):
        adjoint_pair = split(adjoint)
        grad_two = mm(back_out, cat(three(adjoint_pair))) * (1.0 - two * two)
        two_grad_pair = split(grad_two)
        grad_one = mm(back_mid, cat(three(two_grad_pair))) * (1.0 - one * one)
        one_grad_pair = split(grad_one)
        grad_cells = mm(back_in, cat(three(one_grad_pair)))
        left_high = cat([state_pair[0], one_pair[0], adjoint_pair[0], ones])
        left_low = cat([state_pair[1], one_pair[1], adjoint_pair[1], zeros])
        right_high = cat([two_grad_pair[0], one_grad_pair[0], two_pair[0], ones])
        right_low = cat([two_grad_pair[1], one_grad_pair[1], two_pair[1], zeros])
        total[:, 0:208] += mm(left_high, right_high, NT) + (
            mm(left_high, right_low, NT) + mm(left_low, right_high, NT)
        )
        return grad_cells

    def plane(z, carry):
        start = pl.multiple_of(z * 16, 16)
        rows = pl.ds(start, 16)
        rows_cot = pl.ds(pl.multiple_of(256 + z * 16, 16), 16)
        state_zero = s0[rows, :]
        one, one_pair, two, two_pair = layers(go_in0, [state_zero, state_zero, ones])
        rate = mm(go_out, cat(three(two_pair) + [ones]))
        wide_state = state_zero.astype(f32)
        moved = stencil(
            tiles_of(wide_state), x_prev[rows, :].astype(f32), x_next[rows, :].astype(f32),
            tiles_of(moment_ends[rows, :]), z, 1,
        )
        state_one = wide_state + rate - join(moved)
        adjoint = v0[rows, :]
        state_pair = split(state_one)
        saved = layers(go_in1, three(state_pair) + [ones])
        grad_cells = backward(state_pair, *saved, adjoint)
        moved = stencil(
            tiles_of(adjoint), x_prev[rows_cot, :].astype(f32), x_next[rows_cot, :].astype(f32),
            tiles_of(cot_ends[rows, :]), z, 5,
        )
        adjoint = adjoint + grad_cells - join(moved)
        v1_held[rows, :] = adjoint.astype(bf16)
        x_up[rows, :] = adjoint[:, 896:1024].astype(bf16)
        x_down[rows, :] = adjoint[:, 0:128].astype(bf16)
        grad_cells = backward((state_zero, zeros), one, one_pair, two, two_pair, adjoint)
        moved = stencil(tiles_of(adjoint), None, None, None, z, 5)
        part[rows, :] = adjoint + grad_cells - join(moved)
        return carry

    lax.fori_loop(0, 16, plane, 0)
    ends = mm(pick, v1_held[...], NT)
    y_up[...] = ends[0:8]
    y_down[...] = ends[8:16]
    first = total[:, 0:128]
    second = total[:, 128:256]
    turn = lambda item: pltpu.roll(item, 64, 1)
    rest = jnp.concatenate(
        [first[0:16], turn(second[80:96]), first[96:104], turn(first[96:104]), second[80:96]], 0
    )
    sums[...] = jnp.where(iota((64, 128), 1) < 64, first[16:80], rest)


def finish_kernel(part, edge_coefs, x_prev, x_next, y_prev, y_next, out, ends_held):
    pick = edge_picker(8, 1024)
    ends = jnp.concatenate([y_next[...], y_prev[...]], 0).astype(bf16)
    ends_held[...] = mm(ends, pick, TN)
    end_lane = iota((1, 128), 1)

    def plane(z, carry):
        start = pl.multiple_of(z * 16, 16)
        rows = pl.ds(start, 16)
        for x in range(8):
            c = [edge_coefs[pl.ds(k * 128 + z * 8 + x, 1), :] for k in range(4)]
            value = part[rows, x * 128 : x * 128 + 128]
            weight = jnp.where(end_lane == 127, c[2], jnp.where(end_lane == 0, c[3], 0.0))
            value = value + weight * ends_held[rows, x * 128 : x * 128 + 128]
            if x == 7:
                value = value + c[0] * x_next[rows, :].astype(f32)
            if x == 0:
                value = value + c[1] * x_prev[rows, :].astype(f32)
            out[pl.ds(z * 8 + x, 16, stride=128), :] = value
        return carry

    lax.fori_loop(0, 16, plane, 0)


def weights_kernel(scale, mine, other, d_in, d_b_in, d_mid, d_b_mid, d_out, d_b_out):
    value = (mine[...] + other[...]) * scale
    moved = pltpu.roll(value, 64, 1)
    d_mid[...] = value[:, 0:64]
    d_in[...] = moved[0:16, 0:64]
    d_b_in[...] = moved[32:33, 0:64]
    d_b_mid[...] = moved[40:41, 0:64]
    d_out[...] = (moved[16:32, 0:64] * 0.25).T
    d_b_out[...] = (moved[48:64, :] * 0.25).T[0:1, :]


def shifted(block, axis, distance, count):
    route = [(i, i + distance) for i in range(count) if 0 <= i + distance < count]
    return lax.ppermute(block, axis, route)


def pairs(value, axis, links):
    return lax.ppermute(value, axis, [(a, b) for a, b in links] + [(b, a) for a, b in links])


def solution(mesh):
    parts = Mesh(mesh.devices.reshape(4, 4, 4, 2, 2), ("zh", "y", "x", "c", "zl"))
    gx, gy, sa = ("zh", "y"), ("x", "c"), "zl"
    ring = ("zh", "zl")
    wide = P(sa, None, None, gx, gy)
    flat = P(sa, None, gx, gy)
    cells = 4194304
    limit = pltpu.CompilerParams(vmem_limit_bytes=40 * 1024 * 1024)

    def local(moments, speed_x, flag_x, speed_y, flag_y, w_in, b_in, w_mid, b_mid, w_out, b_out, final_cot):
        mom = moments.reshape(2048, 128)
        cot = final_cot.reshape(2048, 128)
        sx, fx, sy, fy = (item.reshape(128, 128) for item in (speed_x, flag_x, speed_y, flag_y))
        shape = jax.ShapeDtypeStruct
        s0, v0, x_up, x_down, y_up, y_down = pl.pallas_call(
            pack_kernel,
            out_shape=(
                shape((256, 1024), bf16), shape((256, 1024), f32),
                shape((544, 128), bf16), shape((512, 128), bf16),
                shape((8, 768), f32), shape((8, 512), f32),
            ),
            scratch_shapes=[pltpu.VMEM((2048, 128), f32), pltpu.VMEM((256, 128), f32)],
            compiler_params=limit,
            name="pack",
        )(mom, cot, sx, fx, sy, fy)
        x_prev = shifted(x_up, gx, 1, 16)
        x_next = shifted(x_down, gx, -1, 16)
        y_prev = shifted(y_up, gy, 1, 8)
        y_next = shifted(y_down, gy, -1, 8)
        part, edge_coefs, x_up, x_down, y_up, y_down, sums = pl.pallas_call(
            main_kernel,
            out_shape=(
                shape((256, 1024), f32), shape((512, 128), f32),
                shape((256, 128), bf16), shape((256, 128), bf16),
                shape((8, 256), f32), shape((8, 256), f32), shape((64, 128), f32),
            ),
            scratch_shapes=[
                pltpu.VMEM((9 * 128, 128), f32), pltpu.VMEM((256, 1024), f32),
                pltpu.VMEM((256, 1024), f32), pltpu.VMEM((256, 1024), bf16),
                pltpu.VMEM((112, 256), f32),
            ],
            compiler_params=limit,
            name="network",
        )(
            s0, v0, sx, fx, sy, fy, x_prev, x_next, y_prev, y_next,
            w_in, b_in.reshape(1, 64), w_mid, b_mid.reshape(1, 64), w_out, b_out.reshape(1, 16),
        )
        x_prev = shifted(x_up, gx, 1, 16)
        x_next = shifted(x_down, gx, -1, 16)
        y_prev = shifted(y_up, gy, 1, 8)
        y_next = shifted(y_down, gy, -1, 8)
        out = pl.pallas_call(
            finish_kernel,
            out_shape=shape((2048, 128), f32),
            scratch_shapes=[pltpu.VMEM((256, 1024), f32)],
            compiler_params=limit,
            name="finish",
        )(part, edge_coefs, x_prev, x_next, y_prev, y_next)

        for axis, links in (
            ("c", [(0, 1)]),
            ("x", [(0, 1), (2, 3)]),
            ("x", [(0, 3), (1, 2)]),
            ("y", [(0, 1), (2, 3)]),
            ("y", [(0, 3), (1, 2)]),
            (ring, [(0, 1), (2, 3), (4, 5), (6, 7)]),
            (ring, [(1, 2), (3, 4), (5, 6), (7, 0)]),
        ):
            sums = sums + pairs(sums, axis, links)
        other = pairs(sums, ring, [(0, 3), (1, 6), (2, 5), (4, 7)])
        grads = pl.pallas_call(
            lambda *refs: weights_kernel(1.0 / cells, *refs),
            out_shape=(
                shape((16, 64), f32), shape((1, 64), f32), shape((64, 64), f32),
                shape((1, 64), f32), shape((64, 16), f32), shape((1, 16), f32),
            ),
            name="weights",
        )(sums, other)
        d_in, d_b_in, d_mid, d_b_mid, d_out, d_b_out = grads
        return (
            out.reshape(final_cot.shape), d_in, d_b_in.reshape(64), d_mid, d_b_mid.reshape(64),
            d_out, d_b_out.reshape(16),
        )

    return jax.shard_map(
        local,
        mesh=parts,
        in_specs=(wide, flat, flat, flat, flat, P(), P(), P(), P(), P(), P(), wide),
        out_specs=(wide, P(), P(), P(), P(), P(), P()),
        check_vma=False,
    )
```

profile of v0, /device:TPU:1, one launch (start us, length us, event | category | flops | bytes accessed | tf_op | source)
XLA Modules:
  0.0 119.6 jit_solution(6318505340963202586)
XLA Ops:
  0.6 1.2 %copy-done = f32[1,16,16,8,128]{4,3,2,1,0:T(8,128)S(1)} copy-done((f32[1,16,16,8,128]{4,3,2,1,0:T(8,128)S(1)}, f32[1,16,16,8,128]{4,3,2,1,0:T(8,128)}, u32[]{:S(2)}) %copy-start) | copy-done | bytes 1048600
  1.9 1.0 copy-done.1
  2.9 0.8 copy-done.2
  3.7 0.8 copy-done.4
  4.6 0.8 copy-done.6
  5.3 0.8 copy-done.8
  6.1 1.8 %pack.1 = (bf16[256,1024]{1,0:T(8,128)(2,1)S(1)}, f32[256,1024]{1,0:T(8,128)S(1)}, bf16[544,128]{1,0:T(8,128)(2,1)S(1)}, bf16[512,128]{1,0:T(8,128)(2,1)S(1)}, f...) custom-call(bf16[2048,128]{1,0:T(8,128)(2,1)S(1)} %bitcast.14, f32[2048,128]{1,0:T(8,128)S(1)} %bitcast.13, ...), custom_call_target="tpu_custom_call" | custom-call | tf_op jit(solution)/shard_map/pack/pallas_call | solution.py:304
  7.9 4.2 %collective-permute-start = (bf16[544,128]{1,0:T(8,128)(2,1)S(1)}, bf16[544,128]{1,0:T(8,128)(2,1)S(1)}, u32[]{:S(2)}, u32[]{:S(2)}) collective-permute-start(bf16[544,128]{1,0:T(8,128)(2,1)S(1)} %get-tuple-element.28), channel_id=1, source_target_pairs={{0,16},{16,32},{32,48},{48,64},{64,80},{80,96},{96,112},{112,128},... | collective-permute-start | bytes 417800 | tf_op jit(solution)/shard_map/ppermute | solution.py:283
  12.1 1.3 %collective-permute-start.1 = (bf16[512,128]{1,0:T(8,128)(2,1)S(1)}, bf16[512,128]{1,0:T(8,128)(2,1)S(1)}, u32[]{:S(2)}, u32[]{:S(2)}) collective-permute-start(bf16[512,128]{1,0:T(8,128)(2,1)S(1)} %get-tuple-element.29), channel_id=1, source_target_pairs={{16,0},{32,16},{48,32},{64,48},{80,64},{96,80},{112,96},{128,112},... | collective-permute-start | bytes 393224 | tf_op jit(solution)/shard_map/ppermute | solution.py:283
  13.4 4.0 %collective-permute-start.2 = (f32[8,768]{1,0:T(8,128)S(1)}, f32[8,768]{1,0:T(8,128)S(1)}, u32[]{:S(2)}, u32[]{:S(2)}) collective-permute-start(f32[8,768]{1,0:T(8,128)S(1)} %get-tuple-element.30), channel_id=1, source_target_pairs={{0,2},{2,4},{4,6},{6,8},{8,10},{10,12},{12,14},{1,3},{3,5},{5,7},{... | collective-permute-start | bytes 73736 | tf_op jit(solution)/shard_map/ppermute | solution.py:283
  17.4 1.9 %collective-permute-start.3 = (f32[8,512]{1,0:T(8,128)S(1)}, f32[8,512]{1,0:T(8,128)S(1)}, u32[]{:S(2)}, u32[]{:S(2)}) collective-permute-start(f32[8,512]{1,0:T(8,128)S(1)} %get-tuple-element.31), channel_id=1, source_target_pairs={{2,0},{4,2},{6,4},{8,6},{10,8},{12,10},{14,12},{3,1},{5,3},{7,5},{... | collective-permute-start | bytes 49160 | tf_op jit(solution)/shard_map/ppermute | solution.py:283
  19.3 0.0 copy-start.14
  19.3 0.1 copy.19.w_out
  19.4 3.0 %collective-permute-done.3.y_next = f32[8,512]{1,0:T(8,128)S(1)} collective-permute-done((f32[8,512]{1,0:T(8,128)S(1)}, f32[8,512]{1,0:T(8,128)S(1)}, u32[]{:S(2)}, u32[]{:S(2)}) %collective-permute-start.3) | collective-permute-done | bytes 16416 | tf_op jit(solution)/shard_map/ppermute | solution.py:283
  22.4 0.0 collective-permute-done.2.y_prev
  22.4 0.0 collective-permute-done.1.x_next
  22.4 0.0 collective-permute-done.x_prev
  22.4 0.0 copy-start.12
  22.4 0.0 copy-start.13
  22.5 0.6 copy-done.12
  23.1 0.0 copy-done.13
  23.1 36.8 %network.1 = (f32[256,1024]{1,0:T(8,128)S(1)}, f32[512,128]{1,0:T(8,128)S(1)}, bf16[256,128]{1,0:T(8,128)(2,1)S(1)}, bf16[256,128]{1,0:T(8,128)(2,1)S(1)}, f32[8...) custom-call(bf16[256,1024]{1,0:T(8,128)(2,1)S(1)} %get-tuple-element.26.s0, ...), custom_call_target="tpu_custom_call" | custom-call | tf_op jit(solution)/shard_map/network/pallas_call | solution.py:319
  59.9 1.2 %collective-permute-done.8 = f32[64,128]{1,0:T(8,128)S(1)} collective-permute-done((f32[64,128]{1,0:T(8,128)S(1)}, f32[64,128]{1,0:T(8,128)S(1)}, u32[]{:S(2)}, u32[]{:S(2)}) %collective-permute-start.8) | collective-permute-done | bytes 32800 | tf_op jit(solution)/shard_map/ppermute | solution.py:287
  61.2 1.2 %collective-permute-start.9 = (f32[64,128]{1,0:T(8,128)S(1)}, f32[64,128]{1,0:T(8,128)S(1)}, u32[]{:S(2)}, u32[]{:S(2)}) collective-permute-start(f32[64,128]{1,0:T(8,128)S(1)} %add.21), channel_id=1, source_target_pairs={{0,4},{8,12},{4,0},{12,8},{1,5},{9,13},{5,1},{13,9},{2,6},{10,14},... | collective-permute-start | bytes 98312 | tf_op jit(solution)/shard_map/ppermute | solution.py:287
  62.4 1.6 %collective-permute-done.9 = f32[64,128]{1,0:T(8,128)S(1)} collective-permute-done((f32[64,128]{1,0:T(8,128)S(1)}, f32[64,128]{1,0:T(8,128)S(1)}, u32[]{:S(2)}, u32[]{:S(2)}) %collective-permute-start.9) | collective-permute-done | bytes 32800 | tf_op jit(solution)/shard_map/ppermute | solution.py:287
  63.9 1.3 %collective-permute-start.10 = (f32[64,128]{1,0:T(8,128)S(1)}, f32[64,128]{1,0:T(8,128)S(1)}, u32[]{:S(2)}, u32[]{:S(2)}) collective-permute-start(f32[64,128]{1,0:T(8,128)S(1)} %add.22), channel_id=1, source_target_pairs={{0,12},{4,8},{12,0},{8,4},{1,13},{5,9},{13,1},{9,5},{2,14},{6,10},... | collective-permute-start | bytes 98312 | tf_op jit(solution)/shard_map/ppermute | solution.py:287
  65.2 2.7 %collective-permute-done.10 = f32[64,128]{1,0:T(8,128)S(1)} collective-permute-done((f32[64,128]{1,0:T(8,128)S(1)}, f32[64,128]{1,0:T(8,128)S(1)}, u32[]{:S(2)}, u32[]{:S(2)}) %collective-permute-start.10) | collective-permute-done | bytes 32800 | tf_op jit(solution)/shard_map/ppermute | solution.py:287
  67.9 2.4 %collective-permute-start.11 = (f32[64,128]{1,0:T(8,128)S(1)}, f32[64,128]{1,0:T(8,128)S(1)}, u32[]{:S(2)}, u32[]{:S(2)}) collective-permute-start(f32[64,128]{1,0:T(8,128)S(1)} %add.23), channel_id=1, source_target_pairs={{0,16},{32,48},{16,0},{48,32},{1,17},{33,49},{17,1},{49,33},{2,18}... | collective-permute-start | bytes 98312 | tf_op jit(solution)/shard_map/ppermute | solution.py:287
  70.3 1.3 %collective-permute-done.11 = f32[64,128]{1,0:T(8,128)S(1)} collective-permute-done((f32[64,128]{1,0:T(8,128)S(1)}, f32[64,128]{1,0:T(8,128)S(1)}, u32[]{:S(2)}, u32[]{:S(2)}) %collective-permute-start.11) | collective-permute-done | bytes 32800 | tf_op jit(solution)/shard_map/ppermute | solution.py:287
  71.6 6.1 %collective-permute-start.12 = (f32[64,128]{1,0:T(8,128)S(1)}, f32[64,128]{1,0:T(8,128)S(1)}, u32[]{:S(2)}, u32[]{:S(2)}) collective-permute-start(f32[64,128]{1,0:T(8,128)S(1)} %add.24), channel_id=1, source_target_pairs={{0,48},{16,32},{48,0},{32,16},{1,49},{17,33},{49,1},{33,17},{2,50}... | collective-permute-start | bytes 98312 | tf_op jit(solution)/shard_map/ppermute | solution.py:287
  77.7 1.3 %collective-permute-done.12 = f32[64,128]{1,0:T(8,128)S(1)} collective-permute-done((f32[64,128]{1,0:T(8,128)S(1)}, f32[64,128]{1,0:T(8,128)S(1)}, u32[]{:S(2)}, u32[]{:S(2)}) %collective-permute-start.12) | collective-permute-done | bytes 32800 | tf_op jit(solution)/shard_map/ppermute | solution.py:287
  79.0 0.0 collective-permute-start.13
  79.0 1.3 %collective-permute-start.4 = (bf16[256,128]{1,0:T(8,128)(2,1)S(1)}, bf16[256,128]{1,0:T(8,128)(2,1)S(1)}, u32[]{:S(2)}, u32[]{:S(2)}) collective-permute-start(bf16[256,128]{1,0:T(8,128)(2,1)S(1)} %get-tuple-element.34), channel_id=1, source_target_pairs={{0,16},{16,32},{32,48},{48,64},{64,80},{80,96},{96,112},{112,128},... | collective-permute-start | bytes 196616 | tf_op jit(solution)/shard_map/ppermute | solution.py:283
  80.3 1.3 %collective-permute-start.5 = (bf16[256,128]{1,0:T(8,128)(2,1)S(1)}, bf16[256,128]{1,0:T(8,128)(2,1)S(1)}, u32[]{:S(2)}, u32[]{:S(2)}) collective-permute-start(bf16[256,128]{1,0:T(8,128)(2,1)S(1)} %get-tuple-element.35), channel_id=1, source_target_pairs={{16,0},{32,16},{48,32},{64,48},{80,64},{96,80},{112,96},{128,112},... | collective-permute-start | bytes 196616 | tf_op jit(solution)/shard_map/ppermute | solution.py:283
  81.6 0.1 collective-permute-done.13
  81.8 11.7 %collective-permute-start.14 = (f32[64,128]{1,0:T(8,128)S(1)}, f32[64,128]{1,0:T(8,128)S(1)}, u32[]{:S(2)}, u32[]{:S(2)}) collective-permute-start(f32[64,128]{1,0:T(8,128)S(1)} %add.26), channel_id=1, source_target_pairs={{1,64},{65,128},{129,192},{193,0},{64,1},{128,65},{192,129},{0,193... | collective-permute-start | bytes 98312 | tf_op jit(solution)/shard_map/ppermute | solution.py:287
  93.4 1.3 %collective-permute-done.14 = f32[64,128]{1,0:T(8,128)S(1)} collective-permute-done((f32[64,128]{1,0:T(8,128)S(1)}, f32[64,128]{1,0:T(8,128)S(1)}, u32[]{:S(2)}, u32[]{:S(2)}) %collective-permute-start.14) | collective-permute-done | bytes 32800 | tf_op jit(solution)/shard_map/ppermute | solution.py:287
  94.8 5.4 %collective-permute-start.15 = (f32[64,128]{1,0:T(8,128)S(1)}, f32[64,128]{1,0:T(8,128)S(1)}, u32[]{:S(2)}, u32[]{:S(2)}) collective-permute-start(f32[64,128]{1,0:T(8,128)S(1)} %add.27.refs_0_), channel_id=1, source_target_pairs={{0,65},{1,192},{64,129},{128,193},{65,0},{192,1},{129,64},{193,128... | collective-permute-start | bytes 98312 | tf_op jit(solution)/shard_map/ppermute | solution.py:287
  100.2 8.5 %collective-permute-start.6 = (f32[8,256]{1,0:T(8,128)S(1)}, f32[8,256]{1,0:T(8,128)S(1)}, u32[]{:S(2)}, u32[]{:S(2)}) collective-permute-start(f32[8,256]{1,0:T(8,128)S(1)} %get-tuple-element.36), channel_id=1, source_target_pairs={{0,2},{2,4},{4,6},{6,8},{8,10},{10,12},{12,14},{1,3},{3,5},{5,7},{... | collective-permute-start | bytes 24584 | tf_op jit(solution)/shard_map/ppermute | solution.py:283
  108.7 1.9 %collective-permute-start.7 = (f32[8,256]{1,0:T(8,128)S(1)}, f32[8,256]{1,0:T(8,128)S(1)}, u32[]{:S(2)}, u32[]{:S(2)}) collective-permute-start(f32[8,256]{1,0:T(8,128)S(1)} %get-tuple-element.37), channel_id=1, source_target_pairs={{2,0},{4,2},{6,4},{8,6},{10,8},{12,10},{14,12},{3,1},{5,3},{7,5},{... | collective-permute-start | bytes 24584 | tf_op jit(solution)/shard_map/ppermute | solution.py:283
  110.6 0.0 collective-permute-done.6.y_prev
  110.6 3.0 %collective-permute-done.7.y_next = f32[8,256]{1,0:T(8,128)S(1)} collective-permute-done((f32[8,256]{1,0:T(8,128)S(1)}, f32[8,256]{1,0:T(8,128)S(1)}, u32[]{:S(2)}, u32[]{:S(2)}) %collective-permute-start.7) | collective-permute-done | bytes 8224 | tf_op jit(solution)/shard_map/ppermute | solution.py:283
  113.7 0.0 collective-permute-done.4.x_prev
  113.7 0.0 collective-permute-done.5.x_next
  113.7 2.3 %finish.1 = f32[2048,128]{1,0:T(8,128)} custom-call(f32[256,1024]{1,0:T(8,128)S(1)} %get-tuple-element.32.part, f32[512,128]{1,0:T(8,128)S(1)} %get-tuple-element.33.edge_coefs, bf16[256,128]{1,0:T(8,128)(2,1)S(1)} %collective-permute-done.4.x_prev, bf16[256,128]{1,0:T(8,128)(2,1)S(1)} %collective-permute-done.5.x_next, ...), custom_call_target="tpu_custom_call" | custom-call | tf_op jit(solution)/shard_map/finish/pallas_call | solution.py:341
  116.0 0.6 copy-done.16
  116.6 1.5 %weights.1 = (f32[16,64]{1,0:T(8,128)}, f32[1,64]{1,0:T(1,128)}, f32[64,64]{1,0:T(8,128)}, f32[1,64]{1,0:T(1,128)}, f32[64,16]{1,0:T(8,128)}, /*index=5*/f32[1,16]{1,0:T(1,128)}) custom-call(f32[64,128]{1,0:T(8,128)} %copy-done.15, f32[64,128]{1,0:T(8,128)} %copy-done.16), custom_call_target="tpu_custom_call" | custom-call | tf_op jit(solution)/shard_map/weights/pallas_call | solution.py:360
  118.2 1.4 %copy.20 = f32[64,16]{0,1:T(8,128)} copy(f32[64,16]{1,0:T(8,128)} %get-tuple-element.50) | data formatting | bytes 8192
  (33 shorter events, 0.1 us)
Async XLA Ops:
  0.6 1.2 %copy-start = (f32[1,16,16,8,128]{4,3,2,1,0:T(8,128)S(1)}, f32[1,16,16,8,128]{4,3,2,1,0:T(8,128)}, u32[]{:S(2)}) copy-start(f32[1,16,16,8,128]{4,3,2,1,0:T(8,128)} %param.23) | copy-start | bytes 3145732
  1.9 1.0 copy-start.1
  2.9 0.8 copy-start.2
  3.7 0.8 copy-start.4
  4.6 0.8 copy-start.6
  5.3 0.8 copy-start.8
  6.1 13.2 %copy-start.17 = (f32[64,16]{0,1:T(8,128)S(1)}, f32[64,16]{0,1:T(8,128)}, u32[]{:S(2)}) copy-start(f32[64,16]{0,1:T(8,128)} %param.21) | copy-start | bytes 12292
  6.1 16.4 %copy-start.3 = (s32[1,16,8,128]{3,2,1,0:T(8,128)S(1)}, s32[1,16,8,128]{3,2,1,0:T(8,128)}, u32[]{:S(2)}) copy-start(s32[1,16,8,128]{3,2,1,0:T(8,128)} %param.14) | copy-start | bytes 196612
  6.1 16.4 %copy-start.5 = (s32[1,16,8,128]{3,2,1,0:T(8,128)S(1)}, s32[1,16,8,128]{3,2,1,0:T(8,128)}, u32[]{:S(2)}) copy-start(s32[1,16,8,128]{3,2,1,0:T(8,128)} %param.16) | copy-start | bytes 196612
  6.1 16.4 %copy-start.9 = (bf16[1,16,8,128]{3,2,1,0:T(8,128)(2,1)S(1)}, bf16[1,16,8,128]{3,2,1,0:T(8,128)(2,1)}, u32[]{:S(2)}) copy-start(bf16[1,16,8,128]{3,2,1,0:T(8,128)(2,1)} %param.15) | copy-start | bytes 98308
  6.1 16.4 %copy-start.10 = (f32[64,64]{1,0:T(8,128)S(1)}, f32[64,64]{1,0:T(8,128)}, u32[]{:S(2)}) copy-start(f32[64,64]{1,0:T(8,128)} %w_mid.1) | copy-start | bytes 49156
  7.9 14.6 %copy-start.7 = (bf16[1,16,8,128]{3,2,1,0:T(8,128)(2,1)S(1)}, bf16[1,16,8,128]{3,2,1,0:T(8,128)(2,1)}, u32[]{:S(2)}) copy-start(bf16[1,16,8,128]{3,2,1,0:T(8,128)(2,1)} %param.13) | copy-start | bytes 98308
  7.9 14.5 %collective-permute-start = (bf16[544,128]{1,0:T(8,128)(2,1)S(1)}, bf16[544,128]{1,0:T(8,128)(2,1)S(1)}, u32[]{:S(2)}, u32[]{:S(2)}) collective-permute-start(bf16[544,128]{1,0:T(8,128)(2,1)S(1)} %get-tuple-element.28), channel_id=1, source_target_pairs={{0,16},{16,32},{32,48},{48,64},{64,80},{80,96},{96,112},{112,128},... | collective-permute-start | bytes 417800 | tf_op jit(solution)/shard_map/ppermute | solution.py:283
  12.1 10.3 %collective-permute-start.1 = (bf16[512,128]{1,0:T(8,128)(2,1)S(1)}, bf16[512,128]{1,0:T(8,128)(2,1)S(1)}, u32[]{:S(2)}, u32[]{:S(2)}) collective-permute-start(bf16[512,128]{1,0:T(8,128)(2,1)S(1)} %get-tuple-element.29), channel_id=1, source_target_pairs={{16,0},{32,16},{48,32},{64,48},{80,64},{96,80},{112,96},{128,112},... | collective-permute-start | bytes 393224 | tf_op jit(solution)/shard_map/ppermute | solution.py:283
  13.4 9.0 %collective-permute-start.2 = (f32[8,768]{1,0:T(8,128)S(1)}, f32[8,768]{1,0:T(8,128)S(1)}, u32[]{:S(2)}, u32[]{:S(2)}) collective-permute-start(f32[8,768]{1,0:T(8,128)S(1)} %get-tuple-element.30), channel_id=1, source_target_pairs={{0,2},{2,4},{4,6},{6,8},{8,10},{10,12},{12,14},{1,3},{3,5},{5,7},{... | collective-permute-start | bytes 73736 | tf_op jit(solution)/shard_map/ppermute | solution.py:283
  17.4 5.1 %collective-permute-start.3 = (f32[8,512]{1,0:T(8,128)S(1)}, f32[8,512]{1,0:T(8,128)S(1)}, u32[]{:S(2)}, u32[]{:S(2)}) collective-permute-start(f32[8,512]{1,0:T(8,128)S(1)} %get-tuple-element.31), channel_id=1, source_target_pairs={{2,0},{4,2},{6,4},{8,6},{10,8},{12,10},{14,12},{3,1},{5,3},{7,5},{... | collective-permute-start | bytes 49160 | tf_op jit(solution)/shard_map/ppermute | solution.py:283
  19.3 3.2 %copy-start.14 = (f32[16]{0:T(128)S(1)}, f32[16]{0:T(128)}, u32[]{:S(2)}) copy-start(f32[16]{0:T(128)} %param.22) | copy-start | bytes 196
  19.4 3.1 %copy-start.11 = (f32[16,64]{1,0:T(8,128)S(1)}, f32[16,64]{1,0:T(8,128)}, u32[]{:S(2)}) copy-start(f32[16,64]{1,0:T(8,128)} %w_in.1) | copy-start | bytes 12292
  22.4 0.7 copy-start.12
  22.4 0.7 copy-start.13
  59.9 1.2 %collective-permute-start.8 = (f32[64,128]{1,0:T(8,128)S(1)}, f32[64,128]{1,0:T(8,128)S(1)}, u32[]{:S(2)}, u32[]{:S(2)}) collective-permute-start(f32[64,128]{1,0:T(8,128)S(1)} %get-tuple-element.38), channel_id=1, source_target_pairs={{0,2},{2,0},{1,3},{3,1},{4,6},{6,4},{5,7},{7,5},{8,10},{10,8},{9,1... | collective-permute-start | bytes 98312 | tf_op jit(solution)/shard_map/ppermute | solution.py:287
  61.2 2.8 %collective-permute-start.9 = (f32[64,128]{1,0:T(8,128)S(1)}, f32[64,128]{1,0:T(8,128)S(1)}, u32[]{:S(2)}, u32[]{:S(2)}) collective-permute-start(f32[64,128]{1,0:T(8,128)S(1)} %add.21), channel_id=1, source_target_pairs={{0,4},{8,12},{4,0},{12,8},{1,5},{9,13},{5,1},{13,9},{2,6},{10,14},... | collective-permute-start | bytes 98312 | tf_op jit(solution)/shard_map/ppermute | solution.py:287
  63.9 4.0 %collective-permute-start.10 = (f32[64,128]{1,0:T(8,128)S(1)}, f32[64,128]{1,0:T(8,128)S(1)}, u32[]{:S(2)}, u32[]{:S(2)}) collective-permute-start(f32[64,128]{1,0:T(8,128)S(1)} %add.22), channel_id=1, source_target_pairs={{0,12},{4,8},{12,0},{8,4},{1,13},{5,9},{13,1},{9,5},{2,14},{6,10},... | collective-permute-start | bytes 98312 | tf_op jit(solution)/shard_map/ppermute | solution.py:287
  67.9 3.7 %collective-permute-start.11 = (f32[64,128]{1,0:T(8,128)S(1)}, f32[64,128]{1,0:T(8,128)S(1)}, u32[]{:S(2)}, u32[]{:S(2)}) collective-permute-start(f32[64,128]{1,0:T(8,128)S(1)} %add.23), channel_id=1, source_target_pairs={{0,16},{32,48},{16,0},{48,32},{1,17},{33,49},{17,1},{49,33},{2,18}... | collective-permute-start | bytes 98312 | tf_op jit(solution)/shard_map/ppermute | solution.py:287
  71.6 7.4 %collective-permute-start.12 = (f32[64,128]{1,0:T(8,128)S(1)}, f32[64,128]{1,0:T(8,128)S(1)}, u32[]{:S(2)}, u32[]{:S(2)}) collective-permute-start(f32[64,128]{1,0:T(8,128)S(1)} %add.24), channel_id=1, source_target_pairs={{0,48},{16,32},{48,0},{32,16},{1,49},{17,33},{49,1},{33,17},{2,50}... | collective-permute-start | bytes 98312 | tf_op jit(solution)/shard_map/ppermute | solution.py:287
  79.0 2.8 %collective-permute-start.13 = (f32[64,128]{1,0:T(8,128)S(1)}, f32[64,128]{1,0:T(8,128)S(1)}, u32[]{:S(2)}, u32[]{:S(2)}) collective-permute-start(f32[64,128]{1,0:T(8,128)S(1)} %add.25), channel_id=1, source_target_pairs={{0,1},{64,65},{128,129},{192,193},{1,0},{65,64},{129,128},{193,192... | collective-permute-start | bytes 98312 | tf_op jit(solution)/shard_map/ppermute | solution.py:287
  79.0 34.6 %collective-permute-start.4 = (bf16[256,128]{1,0:T(8,128)(2,1)S(1)}, bf16[256,128]{1,0:T(8,128)(2,1)S(1)}, u32[]{:S(2)}, u32[]{:S(2)}) collective-permute-start(bf16[256,128]{1,0:T(8,128)(2,1)S(1)} %get-tuple-element.34), channel_id=1, source_target_pairs={{0,16},{16,32},{32,48},{48,64},{64,80},{80,96},{96,112},{112,128},... | collective-permute-start | bytes 196616 | tf_op jit(solution)/shard_map/ppermute | solution.py:283
  80.3 33.3 %collective-permute-start.5 = (bf16[256,128]{1,0:T(8,128)(2,1)S(1)}, bf16[256,128]{1,0:T(8,128)(2,1)S(1)}, u32[]{:S(2)}, u32[]{:S(2)}) collective-permute-start(bf16[256,128]{1,0:T(8,128)(2,1)S(1)} %get-tuple-element.35), channel_id=1, source_target_pairs={{16,0},{32,16},{48,32},{64,48},{80,64},{96,80},{112,96},{128,112},... | collective-permute-start | bytes 196616 | tf_op jit(solution)/shard_map/ppermute | solution.py:283
  81.8 13.0 %collective-permute-start.14 = (f32[64,128]{1,0:T(8,128)S(1)}, f32[64,128]{1,0:T(8,128)S(1)}, u32[]{:S(2)}, u32[]{:S(2)}) collective-permute-start(f32[64,128]{1,0:T(8,128)S(1)} %add.26), channel_id=1, source_target_pairs={{1,64},{65,128},{129,192},{193,0},{64,1},{128,65},{192,129},{0,193... | collective-permute-start | bytes 98312 | tf_op jit(solution)/shard_map/ppermute | solution.py:287
  94.8 21.3 %copy-start.15 = (f32[64,128]{1,0:T(8,128)}, f32[64,128]{1,0:T(8,128)S(1)}, u32[]{:S(2)}) copy-start(f32[64,128]{1,0:T(8,128)S(1)} %add.27.refs_0_) | copy-start | bytes 98308
  94.8 21.3 %collective-permute-start.15 = (f32[64,128]{1,0:T(8,128)S(1)}, f32[64,128]{1,0:T(8,128)S(1)}, u32[]{:S(2)}, u32[]{:S(2)}) collective-permute-start(f32[64,128]{1,0:T(8,128)S(1)} %add.27.refs_0_), channel_id=1, source_target_pairs={{0,65},{1,192},{64,129},{128,193},{65,0},{192,1},{129,64},{193,128... | collective-permute-start | bytes 98312 | tf_op jit(solution)/shard_map/ppermute | solution.py:287
  100.2 10.5 %collective-permute-start.6 = (f32[8,256]{1,0:T(8,128)S(1)}, f32[8,256]{1,0:T(8,128)S(1)}, u32[]{:S(2)}, u32[]{:S(2)}) collective-permute-start(f32[8,256]{1,0:T(8,128)S(1)} %get-tuple-element.36), channel_id=1, source_target_pairs={{0,2},{2,4},{4,6},{6,8},{8,10},{10,12},{12,14},{1,3},{3,5},{5,7},{... | collective-permute-start | bytes 24584 | tf_op jit(solution)/shard_map/ppermute | solution.py:283
  108.7 5.0 %collective-permute-start.7 = (f32[8,256]{1,0:T(8,128)S(1)}, f32[8,256]{1,0:T(8,128)S(1)}, u32[]{:S(2)}, u32[]{:S(2)}) collective-permute-start(f32[8,256]{1,0:T(8,128)S(1)} %get-tuple-element.37), channel_id=1, source_target_pairs={{2,0},{4,2},{6,4},{8,6},{10,8},{12,10},{14,12},{3,1},{5,3},{7,5},{... | collective-permute-start | bytes 24584 | tf_op jit(solution)/shard_map/ppermute | solution.py:283
  116.0 0.6 copy-start.16
where the time goes:
time: 120 us
  starting transfers between devices  52.4 us (44%)
  Pallas kernels  42.5 us (35%)
  waiting for transfers between devices  15.6 us (13%)
  local copies, waits for them, and re-layouts  8.2 us (7%)
    pallas_call x1, Pallas kernels, local(): pl.pallas_call(main_kernel, out_shape=(shape((256, 1024), f32), shape((51...  36.8 us
    ppermute x8, starting transfers between devices, pairs(): lax.ppermute(value, axis, [(a, b) for a, b in links] + [(b, a) for a, b i...  28 us
    ppermute x8, starting transfers between devices, shifted(): return lax.ppermute(block, axis, route)  24.4 us
    ppermute x8, waiting for transfers between devices, pairs(): lax.ppermute(value, axis, [(a, b) for a, b in links] + [(b, a) for a, b i...  9.55 us
    unnamed x38, local copies, waits for them, and re-layouts  8.2 us
    ppermute x8, waiting for transfers between devices, shifted(): return lax.ppermute(block, axis, route)  6.07 us
  transfers between devices with their start and end apart: 16, of which 9 were waited for; matrix products, arithmetic and copies ran while one was open for 0% of the time, Pallas kernels for 2%

commit v1 on v0

v1 whole, which is shorter than its diff:
```python
import jax
import jax.numpy as jnp
from jax import lax
from jax.experimental import pallas as pl
from jax.experimental.pallas import tpu as pltpu
from jax.sharding import Mesh, PartitionSpec as P

f32 = jnp.float32
bf16 = jnp.bfloat16

NN = (((1,), (0,)), ((), ()))
NT = (((1,), (1,)), ((), ()))
TN = (((0,), (0,)), ((), ()))
PLANES = 4
PACK = 56


def mm(a, b, dims=NN):
    return lax.dot_general(a, b, dims, preferred_element_type=f32)


def split(value):
    high = value.astype(bf16)
    return high, (value - high.astype(f32)).astype(bf16)


def iota(shape, dim):
    return lax.broadcasted_iota(jnp.int32, shape, dim)


def edge_picker(rows, length):
    row, lane = iota((2 * rows, length), 0), iota((2 * rows, length), 1)
    spot = jnp.where(row < rows, row * 128 + 127, (row - rows) * 128)
    return jnp.where(lane == spot, 1.0, 0.0).astype(bf16)


def pack_kernel(
    cot_far, mom_far, sx_far, fx_far, sy_far, fy_far,
    w_in_far, b_in_far, w_mid_far, b_mid_far, w_out_far, b_out_far,
    s0, v0, speeds, weights, x_even, x_odd, y_even, y_odd,
    cot, mom, sx, fx, sy, fy, w_in, b_in, w_mid, b_mid, w_out, b_out,
    mom_wide, x_ends, y_ends, sems,
):
    copies = [
        pltpu.make_async_copy(far, near, sems.at[i])
        for i, (far, near) in enumerate(
            (
                (cot_far, cot), (mom_far, mom), (sx_far, sx), (fx_far, fx), (sy_far, sy), (fy_far, fy),
                (w_in_far, w_in), (b_in_far, b_in), (w_mid_far, w_mid),
                (b_mid_far, b_mid), (w_out_far, w_out), (b_out_far, b_out),
            )
        )
    ]
    for copy in copies:
        copy.start()
    for copy in copies[1:]:
        copy.wait()
    mom_wide[...] = mom[...].astype(f32)
    for index, ref in enumerate((sx, fx, sy, fy)):
        speeds[index * 128 : index * 128 + 128, :] = ref[...].astype(f32)
    weights[...] = jnp.zeros((128, 128), f32)
    weights[0:64, 0:64] = w_mid[...]
    weights[64:80, 0:64] = w_in[...]
    weights[80:96, 0:64] = w_out[...]
    weights[96:97, 0:64] = b_in[...]
    weights[104:105, 0:64] = b_mid[...]
    weights[112:113, 0:16] = b_out[...]
    copies[0].wait()

    def plane(z, carry):
        rows = pl.ds(pl.multiple_of(z * 16, 16), 16)
        rows_cot = pl.ds(pl.multiple_of(256 + z * 16, 16), 16)
        for x in range(8):
            tile = mom_wide[pl.ds(z * 8 + x, 16, stride=128), :].astype(bf16)
            other = cot[pl.ds(z * 8 + x, 16, stride=128), :]
            s0[rows, x * 128 : x * 128 + 128] = tile
            v0[rows, x * 128 : x * 128 + 128] = other
            if x in (0, 7):
                side = 0 if x == 7 else 1
                x_ends[side, rows, :] = tile
                x_ends[side, rows_cot, :] = other.astype(bf16)
        return carry

    lax.fori_loop(0, 16, plane, 0)
    x_ends[0, 512:528, :] = speeds[pl.ds(7, 16, stride=8), :].astype(bf16)
    x_ends[0, 528:544, :] = speeds[pl.ds(128 + 7, 16, stride=8), :].astype(bf16)
    x_ends[1, 512:544, :] = jnp.zeros((32, 128), bf16)
    pick = edge_picker(8, 1024)
    ends = mm(pick, s0[...], NT)
    ends_cot = mm(pick, v0[...].astype(bf16), NT)
    for side in (0, 1):
        y_ends[side, :, 0:256] = ends[side * 8 : side * 8 + 8]
        y_ends[side, :, 256:512] = ends_cot[side * 8 : side * 8 + 8]
    last = jnp.where(iota((8, 128), 1) == 127, 1.0, 0.0).astype(bf16)
    y_ends[0, :, 512:640] = mm(last, sy[...], NT)
    y_ends[0, :, 640:768] = mm(last, fy[...].astype(f32).astype(bf16), NT)
    y_ends[1, :, 512:768] = jnp.zeros((8, 256), f32)
    odd_x, odd_y = parities()
    x_even[...] = x_ends[odd_x]
    x_odd[...] = x_ends[1 - odd_x]
    y_even[0:8, :] = y_ends[odd_y]
    y_odd[0:8, :] = y_ends[1 - odd_y]


def parities():
    return lax.rem(lax.axis_index("y"), 2), lax.axis_index("c")


def forward_kernel(s0, weights, ones_all, twos_all, base):
    w_in, b_in, w_mid, b_mid, w_out, b_out = unbundled(weights)
    in_high, in_low = split(w_in[...])
    in_high, in_low = in_high.astype(f32), in_low.astype(f32)
    go_in = turned(jnp.concatenate([in_high, in_low, bias_rows(b_in[...])], 0))
    go_mid = turned(jnp.concatenate([stacked(w_mid[...]), bias_rows(b_mid[...])], 0))
    go_out = turned(jnp.concatenate([stacked((w_out[...] * 0.25).T), bias_rows(b_out[...] * 0.25)], 0))
    ones = jnp.full((16, PLANES * 1024), 1.0, bf16)

    def group(index, carry):
        rows = [pl.ds(pl.multiple_of((index * PLANES + i) * 16, 16), 16) for i in range(PLANES)]
        lanes = pl.ds(pl.multiple_of(index * PLANES * 1024, PLANES * 1024), PLANES * 1024)
        state = join([s0[r, :] for r in rows])
        one = jnp.tanh(mm(go_in, cat([state, state, ones])))
        ones_all[:, lanes] = one
        two = jnp.tanh(mm(go_mid, cat(three(split(one)) + [ones])))
        twos_all[:, lanes] = two
        result = state.astype(f32) + mm(go_out, cat(three(split(two)) + [ones]))
        for i, r in enumerate(rows):
            base[r, :] = result[:, i * 1024 : i * 1024 + 1024]
        return carry

    lax.fori_loop(0, 16 // PLANES, group, 0)


def unbundled(weights):
    return (
        weights.at[64:80, 0:64], weights.at[96:97, 0:64], weights.at[0:64, 0:64],
        weights.at[104:105, 0:64], weights.at[80:96, 0:64], weights.at[112:113, 0:16],
    )


def join(tiles):
    return jnp.concatenate(tiles, 1)


def cat(items):
    return jnp.concatenate(items, 0)


def stacked(matrix):
    high, low = split(matrix)
    high, low = high.astype(f32), low.astype(f32)
    return jnp.concatenate([high, high, low], 0)


def bias_rows(bias):
    first = bias.astype(bf16).astype(f32)
    rest = bias - first
    second = rest.astype(bf16).astype(f32)
    third = rest - second
    row = iota((16, bias.shape[1]), 0)
    return jnp.where(row == 0, first, jnp.where(row == 1, second, jnp.where(row == 2, third, 0.0)))


def turned(matrix):
    return matrix.T.astype(bf16)


def three(pair):
    return [pair[0], pair[1], pair[0]]


def main_kernel(
    ones_all, twos_all, base, s0, v0, speeds, x_odd, x_even, y_even, y_odd,
    weights,
    part, edge_coefs, x_even_out, x_odd_out, y_even_out, y_odd_out, sums,
    coefs, moment_ends, cot_ends, v1_held, total, x_got, y_got, x_ends, y_ends,
):
    w_in, b_in, w_mid, b_mid, w_out, _ = unbundled(weights)
    odd_x, odd_y = parities()
    x_got[1 - odd_x] = x_even[...]
    x_got[odd_x] = x_odd[...]
    y_got[1 - odd_y] = y_even[0:8, :]
    y_got[odd_y] = y_odd[0:8, :]
    x_prev, x_next, y_prev, y_next = x_got.at[0], x_got.at[1], y_got.at[0], y_got.at[1]
    flag = speeds[128:256, :] * 0.25
    speed = speeds[0:128, :]
    push_x, pull_x = speed * flag, speed * (0.25 - flag)
    flag = speeds[384:512, :] * 0.25
    speed = speeds[256:384, :]
    push_y, pull_y = speed * flag, speed * (0.25 - flag)
    row, lane = iota((128, 128), 0), iota((128, 128), 1)
    speed_prev = x_prev[512:528, :].astype(f32)
    flag_prev = x_prev[528:544, :].astype(f32) * 0.25
    wide = lambda item: jnp.broadcast_to(item[:, None, :], (16, 8, 128)).reshape(128, 128)
    first_row = lax.rem(row, 8) == 0
    pushed_x = jnp.where(first_row, wide(speed_prev * flag_prev), pltpu.roll(push_x, 1, 0))
    pulled_x = jnp.where(first_row, wide(speed_prev * (0.25 - flag_prev)), pltpu.roll(pull_x, 1, 0))
    place = jnp.where((iota((8, 128), 0) == 0) & (iota((8, 128), 1) == 0), 1.0, 0.0).astype(bf16)
    speed_prev = mm(y_prev[:, 512:640].astype(bf16), place, TN)
    flag_prev = mm(y_prev[:, 640:768].astype(bf16), place, TN) * 0.25
    pushed_y = jnp.where(lane == 0, speed_prev * flag_prev, pltpu.roll(push_y, 1, 1))
    pulled_y = jnp.where(lane == 0, speed_prev * (0.25 - flag_prev), pltpu.roll(pull_y, 1, 1))
    keep = push_x + pulled_x + push_y + pulled_y
    for index, item in enumerate(
        (keep, pull_x, pushed_x, pull_y, pushed_y, push_x, pulled_x, push_y, pulled_y)
    ):
        coefs[index * 128 : index * 128 + 128, :] = item
    for index, item in enumerate((push_x, pulled_x, push_y, pulled_y)):
        edge_coefs[index * 128 : index * 128 + 128, :] = item

    pick = edge_picker(8, 1024)
    ends = jnp.concatenate([y_next[:, 0:512], y_prev[:, 0:512]], 0).astype(bf16)
    moment_ends[...] = mm(ends[:, 0:256], pick, TN)
    cot_ends[...] = mm(ends[:, 256:512], pick, TN)

    w_in_, w_mid_ = w_in[...], w_mid[...]
    go_in = turned(jnp.concatenate([stacked(w_in_), bias_rows(b_in[...])], 0))
    go_mid = turned(jnp.concatenate([stacked(w_mid_), bias_rows(b_mid[...])], 0))
    back_out = turned(stacked(w_out[...] * 0.25))
    back_mid = turned(stacked(w_mid_.T))
    back_in = turned(stacked(w_in_.T))
    ones = jnp.full((16, PLANES * 1024), 1.0, bf16)
    zeros = jnp.zeros((16, PLANES * 1024), bf16)
    total[...] = jnp.zeros_like(total)
    end_lane = iota((16, 128), 1)

    def stencil(tiles, before, after, ends, z, first):
        around = [before] + tiles + [after]
        results = []
        for x in range(8):
            c = [
                coefs[pl.ds(k * 128 + z * 8 + x, 1), :] for k in (0, first, first + 1, first + 2, first + 3)
            ]
            here = around[x + 1]
            value = c[0] * here
            if around[x + 2] is not None:
                value = value - c[1] * around[x + 2]
            if around[x] is not None:
                value = value - c[2] * around[x]
            right, left = pltpu.roll(here, 127, 1), pltpu.roll(here, 1, 1)
            if ends is None:
                end = 0.0
            else:
                end = ends[x]
            right = jnp.where(end_lane == 127, end, right)
            left = jnp.where(end_lane == 0, end, left)
            value = value - c[3] * right - c[4] * left
            results.append(value)
        return results

    def tiles_of(value):
        return [value[:, x * 128 : x * 128 + 128] for x in range(8)]

    def layers(inputs):
        one = jnp.tanh(mm(go_in, cat(inputs)))
        one_pair = split(one)
        two = jnp.tanh(mm(go_mid, cat(three(one_pair) + [ones])))
        return one, one_pair, two, split(two)

    def backward(state_pair, one, one_pair, two, two_pair, adjoint):
        adjoint_pair = split(adjoint)
        grad_two = mm(back_out, cat(three(adjoint_pair))) * (1.0 - two * two)
        two_grad_pair = split(grad_two)
        grad_one = mm(back_mid, cat(three(two_grad_pair))) * (1.0 - one * one)
        one_grad_pair = split(grad_one)
        grad_cells = mm(back_in, cat(three(one_grad_pair)))
        left_high = cat([state_pair[0], one_pair[0], adjoint_pair[0], ones])
        left_low = cat([state_pair[1], one_pair[1], adjoint_pair[1], zeros])
        right_high = cat([two_grad_pair[0], one_grad_pair[0], two_pair[0], ones])
        right_low = cat([two_grad_pair[1], one_grad_pair[1], two_pair[1], zeros])
        both = mm(cat([left_high, left_low]), right_high, NT)
        total[:, 0:208] += both[0:112] + both[112:224] + mm(left_high, right_low, NT)
        return grad_cells

    def group(index, carry):
        planes = [index * PLANES + i for i in range(PLANES)]
        rows = [pl.ds(pl.multiple_of(z * 16, 16), 16) for z in planes]
        rows_cot = [pl.ds(pl.multiple_of(256 + z * 16, 16), 16) for z in planes]

        def moves(value, ends, edges, first):
            results = []
            for i, z in enumerate(planes):
                tiles = tiles_of(value[:, i * 1024 : i * 1024 + 1024])
                if ends is None:
                    results += stencil(tiles, None, None, None, z, first)
                else:
                    before, after = (ref[edges[i], :].astype(f32) for ref in (x_prev, x_next))
                    results += stencil(tiles, before, after, tiles_of(ends[rows[i], :]), z, first)
            return join(results)

        state_zero = join([s0[r, :] for r in rows])
        wide_state = state_zero.astype(f32)
        state_one = join([base[r, :] for r in rows]) - moves(wide_state, moment_ends, rows, 1)
        adjoint = join([v0[r, :] for r in rows])
        state_pair = split(state_one)
        saved = layers(three(state_pair) + [ones])
        grad_cells = backward(state_pair, *saved, adjoint)
        adjoint = adjoint + grad_cells - moves(adjoint, cot_ends, rows_cot, 5)
        for i, r in enumerate(rows):
            tile = adjoint[:, i * 1024 : i * 1024 + 1024]
            v1_held[r, :] = tile.astype(bf16)
            x_ends[0, r, :] = tile[:, 896:1024].astype(bf16)
            x_ends[1, r, :] = tile[:, 0:128].astype(bf16)
        lanes = pl.ds(pl.multiple_of(index * PLANES * 1024, PLANES * 1024), PLANES * 1024)
        one, two = ones_all[:, lanes], twos_all[:, lanes]
        grad_cells = backward((state_zero, zeros), one, split(one), two, split(two), adjoint)
        result = adjoint + grad_cells - moves(adjoint, None, None, 5)
        for i, r in enumerate(rows):
            part[r, :] = result[:, i * 1024 : i * 1024 + 1024]
        return carry

    lax.fori_loop(0, 16 // PLANES, group, 0)
    ends = mm(pick, v1_held[...], NT)
    y_ends[0] = ends[0:8]
    y_ends[1] = ends[8:16]
    x_even_out[...] = x_ends[odd_x]
    x_odd_out[...] = x_ends[1 - odd_x]
    y_even_out[...] = y_ends[odd_y]
    y_odd_out[...] = y_ends[1 - odd_y]
    first = total[:, 0:128]
    second = total[:, 128:256]
    turn = lambda item: pltpu.roll(item, 64, 1)
    rest = jnp.concatenate(
        [first[0:16], turn(second[80:96]), first[96:104], turn(first[96:104]), second[80:96]], 0
    )
    sums[...] = jnp.where(iota((64, 128), 1) < 64, first[16:80], rest)


def finish_kernel(part, edge_coefs, x_even, x_odd, y_even, y_odd, out, ends_held, x_got, y_got):
    odd_x, odd_y = parities()
    x_got[1 - odd_x] = x_even[...]
    x_got[odd_x] = x_odd[...]
    y_got[1 - odd_y] = y_even[...]
    y_got[odd_y] = y_odd[...]
    x_prev, x_next, y_prev, y_next = x_got.at[0], x_got.at[1], y_got.at[0], y_got.at[1]
    pick = edge_picker(8, 1024)
    ends = jnp.concatenate([y_next[...], y_prev[...]], 0).astype(bf16)
    ends_held[...] = mm(ends, pick, TN)
    end_lane = iota((1, 128), 1)

    def plane(z, carry):
        start = pl.multiple_of(z * 16, 16)
        rows = pl.ds(start, 16)
        for x in range(8):
            c = [edge_coefs[pl.ds(k * 128 + z * 8 + x, 1), :] for k in range(4)]
            value = part[rows, x * 128 : x * 128 + 128]
            weight = jnp.where(end_lane == 127, c[2], jnp.where(end_lane == 0, c[3], 0.0))
            value = value + weight * ends_held[rows, x * 128 : x * 128 + 128]
            if x == 7:
                value = value + c[0] * x_next[rows, :].astype(f32)
            if x == 0:
                value = value + c[1] * x_prev[rows, :].astype(f32)
            out[pl.ds(z * 8 + x, 16, stride=128), :] = value
        return carry

    lax.fori_loop(0, 16, plane, 0)


def weights_kernel(scale, mine, other, d_in, d_b_in, d_mid, d_b_mid, d_out, d_b_out):
    value = (mine[...] + other[...]) * scale
    moved = pltpu.roll(value, 64, 1)
    d_mid[...] = value[:, 0:64]
    d_in[...] = moved[0:16, 0:64]
    d_b_in[...] = moved[32:33, 0:64]
    d_b_mid[...] = moved[40:41, 0:64]
    d_out[...] = moved[16:32, 0:64] * 0.25
    d_b_out[...] = (moved[48:64, :] * 0.25).T[0:1, :]


def pairs(value, axis, links):
    return lax.ppermute(value, axis, [(a, b) for a, b in links] + [(b, a) for a, b in links])


def swapped(even, odd, axis, count):
    far = pairs(odd, axis, [(i, i + 1) for i in range(1, count - 1, 2)])
    return pairs(even, axis, [(i, i + 1) for i in range(0, count - 1, 2)]), far


def params(mebibytes):
    return pltpu.CompilerParams(vmem_limit_bytes=mebibytes * 1024 * 1024)


def cost(flops, size):
    return pl.CostEstimate(flops=flops, bytes_accessed=size, transcendentals=0)


def solution(mesh):
    parts = Mesh(mesh.devices.reshape(4, 4, 4, 2, 2), ("zh", "y", "x", "c", "zl"))
    gx, gy, sa = ("zh", "y"), ("x", "c"), "zl"
    ring = ("zh", "zl")
    wide = P(sa, None, None, gx, gy)
    flat = P(sa, None, gx, gy)
    cells = 4194304
    far = pl.BlockSpec(memory_space=pltpu.HBM)
    shape = jax.ShapeDtypeStruct

    def local(moments, speed_x, flag_x, speed_y, flag_y, w_in, b_in, w_mid, b_mid, w_out, b_out, final_cot):
        mom = moments.reshape(2048, 128)
        cot = final_cot.reshape(2048, 128)
        sx, fx, sy, fy = (item.reshape(128, 128) for item in (speed_x, flag_x, speed_y, flag_y))
        b_in, b_mid, b_out = b_in.reshape(1, 64), b_mid.reshape(1, 64), b_out.reshape(1, 16)
        w_out = w_out.T
        s0, v0, speeds, bundle, x_even, x_odd, y_even, y_odd = pl.pallas_call(
            pack_kernel,
            in_specs=[far] * 12,
            out_shape=(
                shape((256, 1024), bf16), shape((256, 1024), f32), shape((512, 128), f32),
                shape((128, 128), f32), shape((544, 128), bf16), shape((544, 128), bf16),
                shape((48, 768), f32), shape((48, 768), f32),
            ),
            scratch_shapes=[
                pltpu.VMEM((2048, 128), f32), pltpu.VMEM((2048, 128), bf16),
                pltpu.VMEM((128, 128), bf16), pltpu.VMEM((128, 128), jnp.int32),
                pltpu.VMEM((128, 128), bf16), pltpu.VMEM((128, 128), jnp.int32),
                pltpu.VMEM((16, 64), f32), pltpu.VMEM((1, 64), f32), pltpu.VMEM((64, 64), f32),
                pltpu.VMEM((1, 64), f32), pltpu.VMEM((16, 64), f32), pltpu.VMEM((1, 16), f32),
                pltpu.VMEM((2048, 128), f32), pltpu.VMEM((2, 544, 128), bf16),
                pltpu.VMEM((2, 8, 768), f32), pltpu.SemaphoreType.DMA((12,)),
            ],
            compiler_params=params(PACK),
            name="pack",
        )(cot, mom, sx, fx, sy, fy, w_in, b_in, w_mid, b_mid, w_out, b_out)
        x_even, x_odd = swapped(x_even, x_odd, gx, 16)
        y_even, y_odd = swapped(y_even, y_odd, gy, 8)
        ones_all, twos_all, base = pl.pallas_call(
            forward_kernel,
            out_shape=(shape((64, 16384), f32), shape((64, 16384), f32), shape((256, 1024), f32)),
            compiler_params=params(24),
            cost_estimate=cost(5000000000, 16000000),
            name="forward",
        )(s0, bundle)
        part, edge_coefs, x_even, x_odd, y_even, y_odd, sums = pl.pallas_call(
            main_kernel,
            out_shape=(
                shape((256, 1024), f32), shape((512, 128), f32),
                shape((256, 128), bf16), shape((256, 128), bf16),
                shape((8, 256), f32), shape((8, 256), f32), shape((64, 128), f32),
            ),
            scratch_shapes=[
                pltpu.VMEM((9 * 128, 128), f32), pltpu.VMEM((256, 1024), f32),
                pltpu.VMEM((256, 1024), f32), pltpu.VMEM((256, 1024), bf16),
                pltpu.VMEM((112, 256), f32), pltpu.VMEM((2, 544, 128), bf16),
                pltpu.VMEM((2, 8, 768), f32), pltpu.VMEM((2, 256, 128), bf16),
                pltpu.VMEM((2, 8, 256), f32),
            ],
            compiler_params=params(32),
            cost_estimate=cost(15000000000, 40000000),
            name="network",
        )(
            ones_all, twos_all, base, s0, v0, speeds, x_odd, x_even, y_even, y_odd, bundle
        )
        steps = (
            ("c", [(0, 1)]),
            ("x", [(0, 1), (2, 3)]),
            ("x", [(0, 3), (1, 2)]),
            ("y", [(0, 1), (2, 3)]),
            ("y", [(0, 3), (1, 2)]),
            (ring, [(0, 1), (2, 3), (4, 5), (6, 7)]),
            (ring, [(1, 2), (3, 4), (5, 6), (7, 0)]),
        )
        places = {
            "y_odd": (gy, y_odd, [(1, 2), (3, 4), (5, 6)]),
            "y_even": (gy, y_even, [(0, 1), (2, 3), (4, 5), (6, 7)]),
            "x_even": (gx, x_even, [(i, i + 1) for i in range(0, 15, 2)]),
            "x_odd": (gx, x_odd, [(i, i + 1) for i in range(1, 15, 2)]),
        }
        beside = {1: ("y_odd",), 2: ("y_even",), 3: ("x_even",), 4: ("x_odd",)}
        got = {}
        for index, (axis, links) in enumerate(steps):
            moving = {}
            for name in beside.get(index, ()):
                along, value, route = places[name]
                value, sums = lax.optimization_barrier((value, sums))
                moving[name] = pairs(value, along, route)
            sums = sums + pairs(sums, axis, links)
            if moving:
                names = list(moving)
                *values, sums = lax.optimization_barrier(tuple(moving[n] for n in names) + (sums,))
                got.update(zip(names, values))
        other = pairs(sums, ring, [(0, 3), (1, 6), (2, 5), (4, 7)])
        x_even, x_odd, y_even, y_odd = (got[n] for n in ("x_even", "x_odd", "y_even", "y_odd"))
        out = pl.pallas_call(
            finish_kernel,
            out_shape=shape((2048, 128), f32),
            scratch_shapes=[
                pltpu.VMEM((256, 1024), f32), pltpu.VMEM((2, 256, 128), bf16), pltpu.VMEM((2, 8, 256), f32)
            ],
            compiler_params=params(16),
            cost_estimate=cost(10000000, 6000000),
            name="finish",
        )(part, edge_coefs, x_even, x_odd, y_even, y_odd)

        d_in, d_b_in, d_mid, d_b_mid, d_out, d_b_out = pl.pallas_call(
            lambda *refs: weights_kernel(1.0 / cells, *refs),
            out_shape=(
                shape((16, 64), f32), shape((1, 64), f32), shape((64, 64), f32),
                shape((1, 64), f32), shape((16, 64), f32), shape((1, 16), f32),
            ),
            compiler_params=params(16),
            name="weights",
        )(sums, other)
        return (
            out.reshape(final_cot.shape), d_in, d_b_in.reshape(64), d_mid, d_b_mid.reshape(64),
            d_out.T, d_b_out.reshape(16),
        )

    return jax.shard_map(
        local,
        mesh=parts,
        in_specs=(wide, flat, flat, flat, flat, P(), P(), P(), P(), P(), P(), wide),
        out_specs=(wide, P(), P(), P(), P(), P(), P()),
        check_vma=False,
    )
```

time: 120 us -> 81.1 us (0.68)
  the two profiles are of different devices: /device:TPU:1 before, /device:TPU:30 now
where the time goes in v1:
time: 81.1 us; the launch traced here: 80.8 us
  starting transfers between devices  29.9 us (37%)
  Pallas kernels  26.7 us (33%)
  waiting for transfers between devices  21.5 us (27%)
  local copies, waits for them, and re-layouts  1.89 us (2%)
    ppermute x16, starting transfers between devices, pairs(): lax.ppermute(value, axis, [(a, b) for a, b in links] + [(b, a) for a, b i...  29.9 us
    ppermute x16, waiting for transfers between devices, pairs(): lax.ppermute(value, axis, [(a, b) for a, b in links] + [(b, a) for a, b i...  21.5 us
    pallas_call x1, Pallas kernels, local(): pl.pallas_call(main_kernel, out_shape=(shape((256, 1024), f32), shape((51...  15.8 us
    pallas_call x1, Pallas kernels, local(): pl.pallas_call(pack_kernel, in_specs=[far] * 12, out_shape=(shape((256, 1...  4.33 us
    pallas_call x1, Pallas kernels, local(): pl.pallas_call(forward_kernel, out_shape=(shape((64, 16384), f32), shape(...  3.48 us
    pallas_call x1, Pallas kernels, local(): pl.pallas_call(finish_kernel, out_shape=shape((2048, 128), f32), scratch_...  2.33 us
    unnamed x12, local copies, waits for them, and re-layouts  1.89 us
  transfers between devices with their start and end apart: 16, of which 9 were waited for; matrix products, arithmetic and copies ran while one was open for 0% of the time, Pallas kernels for 7%

profile of v1, /device:TPU:30, one launch (start us, length us, event | category | flops | bytes accessed | tf_op | source)
XLA Modules:
  0.0 80.8 jit_solution(8366495096290045896)
XLA Ops:
  0.6 4.3 %pack.1 = (bf16[256,1024]{1,0:T(8,128)(2,1)}, f32[256,1024]{1,0:T(8,128)}, f32[512,128]{1,0:T(8,128)}, f32[128,128]{1,0:T(8,128)}, bf16[544,128]{1,0:T(8,128)(2,...) custom-call(f32[2048,128]{1,0:T(8,128)} %bitcast.15, bf16[2048,128]{1,0:T(8,128)(2,1)} %bitcast.17, ...), custom_call_target="tpu_custom_call" | custom-call | tf_op jit(solution)/shard_map/pack/pallas_call | solution.py:403
  5.0 4.8 %collective-permute-start = (bf16[544,128]{1,0:T(8,128)(2,1)}, bf16[544,128]{1,0:T(8,128)(2,1)S(1)}, u32[]{:S(2)}, u32[]{:S(2)}) collective-permute-start(bf16[544,128]{1,0:T(8,128)(2,1)} %get-tuple-element.54), channel_id=1, source_target_pairs={{16,32},{48,64},{80,96},{112,128},{144,160},{176,192},{208,224},{3... | collective-permute-start | bytes 417800 | tf_op jit(solution)/shard_map/ppermute | solution.py:371
  9.8 0.1 collective-permute-start.1
  9.9 0.1 collective-permute-start.2
  10.0 2.8 %collective-permute-start.3 = (f32[48,768]{1,0:T(8,128)}, f32[48,768]{1,0:T(8,128)S(1)}, u32[]{:S(2)}, u32[]{:S(2)}) collective-permute-start(f32[48,768]{1,0:T(8,128)} %get-tuple-element.57), channel_id=1, source_target_pairs={{2,4},{6,8},{10,12},{4,2},{8,6},{12,10},{3,5},{7,9},{11,13},{5,3},... | collective-permute-start | bytes 442376 | tf_op jit(solution)/shard_map/ppermute | solution.py:371
  12.9 0.0 copy-start.1
  12.9 1.0 %copy-done.1 = bf16[256,1024]{1,0:T(8,128)(2,1)S(1)} copy-done((bf16[256,1024]{1,0:T(8,128)(2,1)S(1)}, bf16[256,1024]{1,0:T(8,128)(2,1)}, u32[]{:S(2)}) %copy-start.1) | copy-done | bytes 524312
  13.9 0.0 copy-start.4
  13.9 0.8 %copy-done.4 = f32[128,128]{1,0:T(8,128)S(1)} copy-done((f32[128,128]{1,0:T(8,128)S(1)}, f32[128,128]{1,0:T(8,128)}, u32[]{:S(2)}) %copy-start.4) | copy-done | bytes 65560
  14.7 0.0 copy-start
  14.7 0.0 copy-start.2
  14.7 0.0 copy-start.3
  14.7 3.5 %forward.1 = (f32[64,16384]{1,0:T(8,128)S(1)}, f32[64,16384]{1,0:T(8,128)S(1)}, f32[256,1024]{1,0:T(8,128)S(1)}) custom-call(bf16[256,1024]{1,0:T(8,128)(2,1)S(1)} %copy-done.1, f32[128,128]{1,0:T(8,128)S(1)} %copy-done.4), custom_call_target="tpu_custom_call" | custom-call | flops 5000000000 | bytes 16000000 | tf_op jit(solution)/shard_map/forward/pallas_call | solution.py:425
  18.2 0.3 collective-permute-done.x_odd
  18.5 0.0 collective-permute-done.1.x_even
  18.5 0.0 collective-permute-done.2.y_even
  18.5 0.0 collective-permute-done.3.y_odd
  18.5 0.0 copy-done
  18.5 0.0 copy-done.2
  18.5 0.0 copy-done.3
  18.5 0.0 copy-done.5
  18.5 15.8 %network.1 = (f32[256,1024]{1,0:T(8,128)S(1)}, f32[512,128]{1,0:T(8,128)S(1)}, bf16[256,128]{1,0:T(8,128)(2,1)S(1)}, bf16[256,128]{1,0:T(8,128)(2,1)S(1)}, f32[8...) custom-call(f32[64,16384]{1,0:T(8,128)S(1)} %get-tuple-element.49.ones_all, ...), custom_call_target="tpu_custom_call" | custom-call | flops 15000000512 | bytes 40000000 | tf_op jit(solution)/shard_map/network/pallas_call | solution.py:432
  34.4 0.0 collective-permute-start.4
  34.4 1.2 %collective-permute-done.4 = f32[64,128]{1,0:T(8,128)S(1)} collective-permute-done((f32[64,128]{1,0:T(8,128)S(1)}, f32[64,128]{1,0:T(8,128)S(1)}, u32[]{:S(2)}, u32[]{:S(2)}) %collective-permute-start.4) | collective-permute-done | bytes 32800 | tf_op jit(solution)/shard_map/ppermute | solution.py:371
  35.6 0.8 %collective-permute-start.6 = (f32[64,128]{1,0:T(8,128)S(1)}, f32[64,128]{1,0:T(8,128)S(1)}, u32[]{:S(2)}, u32[]{:S(2)}) collective-permute-start(f32[64,128]{1,0:T(8,128)S(1)} %add.21), channel_id=1, source_target_pairs={{0,4},{8,12},{4,0},{12,8},{1,5},{9,13},{5,1},{13,9},{2,6},{10,14},... | collective-permute-start | bytes 98312 | tf_op jit(solution)/shard_map/ppermute | solution.py:371
  36.5 2.6 %collective-permute-start.5 = (f32[8,256]{1,0:T(8,128)S(1)}, f32[8,256]{1,0:T(8,128)S(1)}, u32[]{:S(2)}, u32[]{:S(2)}) collective-permute-start(f32[8,256]{1,0:T(8,128)S(1)} %get-tuple-element.64), channel_id=1, source_target_pairs={{2,4},{6,8},{10,12},{4,2},{8,6},{12,10},{3,5},{7,9},{11,13},{5,3},... | collective-permute-start | bytes 24584 | tf_op jit(solution)/shard_map/ppermute | solution.py:371
  39.0 0.5 collective-permute-done.6
  39.5 1.9 %collective-permute-done.5.y_odd = f32[8,256]{1,0:T(8,128)S(1)} collective-permute-done((f32[8,256]{1,0:T(8,128)S(1)}, f32[8,256]{1,0:T(8,128)S(1)}, u32[]{:S(2)}, u32[]{:S(2)}) %collective-permute-start.5) | collective-permute-done | bytes 8224 | tf_op jit(solution)/shard_map/ppermute | solution.py:371
  41.4 0.0 collective-permute-start.8
  41.4 1.0 %collective-permute-start.7 = (f32[8,256]{1,0:T(8,128)S(1)}, f32[8,256]{1,0:T(8,128)S(1)}, u32[]{:S(2)}, u32[]{:S(2)}) collective-permute-start(f32[8,256]{1,0:T(8,128)S(1)} %get-tuple-element.67), channel_id=1, source_target_pairs={{0,2},{4,6},{8,10},{12,14},{2,0},{6,4},{10,8},{14,12},{1,3},{5,7},... | collective-permute-start | bytes 24584 | tf_op jit(solution)/shard_map/ppermute | solution.py:371
  42.4 4.1 %collective-permute-done.8 = f32[64,128]{1,0:T(8,128)S(1)} collective-permute-done((f32[64,128]{1,0:T(8,128)S(1)}, f32[64,128]{1,0:T(8,128)S(1)}, u32[]{:S(2)}, u32[]{:S(2)}) %collective-permute-start.8) | collective-permute-done | bytes 32800 | tf_op jit(solution)/shard_map/ppermute | solution.py:371
  46.5 0.0 collective-permute-done.7.y_even
  46.5 1.8 %collective-permute-start.9 = (bf16[256,128]{1,0:T(8,128)(2,1)S(1)}, bf16[256,128]{1,0:T(8,128)(2,1)S(1)}, u32[]{:S(2)}, u32[]{:S(2)}) collective-permute-start(bf16[256,128]{1,0:T(8,128)(2,1)S(1)} %get-tuple-element.70), channel_id=1, source_target_pairs={{0,16},{32,48},{64,80},{96,112},{128,144},{160,176},{192,208},{224... | collective-permute-start | bytes 196616 | tf_op jit(solution)/shard_map/ppermute | solution.py:371
  48.4 0.3 collective-permute-start.10
  48.7 3.6 %collective-permute-done.10 = f32[64,128]{1,0:T(8,128)S(1)} collective-permute-done((f32[64,128]{1,0:T(8,128)S(1)}, f32[64,128]{1,0:T(8,128)S(1)}, u32[]{:S(2)}, u32[]{:S(2)}) %collective-permute-start.10) | collective-permute-done | bytes 32800 | tf_op jit(solution)/shard_map/ppermute | solution.py:371
  52.3 0.0 collective-permute-done.9.x_even
  52.3 4.0 %collective-permute-start.11 = (bf16[256,128]{1,0:T(8,128)(2,1)S(1)}, bf16[256,128]{1,0:T(8,128)(2,1)S(1)}, u32[]{:S(2)}, u32[]{:S(2)}) collective-permute-start(bf16[256,128]{1,0:T(8,128)(2,1)S(1)} %get-tuple-element.75), channel_id=1, source_target_pairs={{16,32},{48,64},{80,96},{112,128},{144,160},{176,192},{208,224},{3... | collective-permute-start | bytes 196616 | tf_op jit(solution)/shard_map/ppermute | solution.py:371
  56.3 0.1 collective-permute-start.12
  56.4 5.4 %collective-permute-done.12 = f32[64,128]{1,0:T(8,128)S(1)} collective-permute-done((f32[64,128]{1,0:T(8,128)S(1)}, f32[64,128]{1,0:T(8,128)S(1)}, u32[]{:S(2)}, u32[]{:S(2)}) %collective-permute-start.12) | collective-permute-done | bytes 32800 | tf_op jit(solution)/shard_map/ppermute | solution.py:371
  61.8 0.0 collective-permute-done.11.x_odd
  61.8 2.0 %collective-permute-start.13 = (f32[64,128]{1,0:T(8,128)S(1)}, f32[64,128]{1,0:T(8,128)S(1)}, u32[]{:S(2)}, u32[]{:S(2)}) collective-permute-start(f32[64,128]{1,0:T(8,128)S(1)} %add.25), channel_id=1, source_target_pairs={{0,1},{64,65},{128,129},{192,193},{1,0},{65,64},{129,128},{193,192... | collective-permute-start | bytes 98312 | tf_op jit(solution)/shard_map/ppermute | solution.py:371
  63.8 2.0 %collective-permute-done.13 = f32[64,128]{1,0:T(8,128)S(1)} collective-permute-done((f32[64,128]{1,0:T(8,128)S(1)}, f32[64,128]{1,0:T(8,128)S(1)}, u32[]{:S(2)}, u32[]{:S(2)}) %collective-permute-start.13) | collective-permute-done | bytes 32800 | tf_op jit(solution)/shard_map/ppermute | solution.py:371
  65.8 2.6 %collective-permute-start.14 = (f32[64,128]{1,0:T(8,128)S(1)}, f32[64,128]{1,0:T(8,128)S(1)}, u32[]{:S(2)}, u32[]{:S(2)}) collective-permute-start(f32[64,128]{1,0:T(8,128)S(1)} %add.26), channel_id=1, source_target_pairs={{1,64},{65,128},{129,192},{193,0},{64,1},{128,65},{192,129},{0,193... | collective-permute-start | bytes 98312 | tf_op jit(solution)/shard_map/ppermute | solution.py:371
  68.4 2.6 %collective-permute-done.14 = f32[64,128]{1,0:T(8,128)S(1)} collective-permute-done((f32[64,128]{1,0:T(8,128)S(1)}, f32[64,128]{1,0:T(8,128)S(1)}, u32[]{:S(2)}, u32[]{:S(2)}) %collective-permute-start.14) | collective-permute-done | bytes 32800 | tf_op jit(solution)/shard_map/ppermute | solution.py:371
  71.0 6.8 %collective-permute-start.15 = (f32[64,128]{1,0:T(8,128)S(1)}, f32[64,128]{1,0:T(8,128)S(1)}, u32[]{:S(2)}, u32[]{:S(2)}) collective-permute-start(f32[64,128]{1,0:T(8,128)S(1)} %add.27.refs_0_), channel_id=1, source_target_pairs={{0,65},{1,192},{64,129},{128,193},{65,0},{192,1},{129,64},{193,128... | collective-permute-start | bytes 98312 | tf_op jit(solution)/shard_map/ppermute | solution.py:371
  77.8 2.3 %finish.1 = f32[2048,128]{1,0:T(8,128)} custom-call(f32[256,1024]{1,0:T(8,128)S(1)} %get-tuple-element.58.part, f32[512,128]{1,0:T(8,128)S(1)} %get-tuple-element.59.edge_coefs, bf16[256,128]{1,0:T(8,128)(2,1)S(1)} %collective-permute-done.9.x_even, bf16[256,128]{1,0:T(8,128)(2,1)S(1)} %collective-permute-done.11.x_odd, ...), custom_call_target="tpu_custom_call" | custom-call | flops 10000000 | bytes 6000000 | tf_op jit(solution)/shard_map/finish/pallas_call | solution.py:482
  80.1 0.0 collective-permute-done.15.refs_1_
  80.1 0.7 weights.1
  (8 shorter events, 0.0 us)
Async XLA Ops:
  5.0 13.5 %collective-permute-start = (bf16[544,128]{1,0:T(8,128)(2,1)}, bf16[544,128]{1,0:T(8,128)(2,1)S(1)}, u32[]{:S(2)}, u32[]{:S(2)}) collective-permute-start(bf16[544,128]{1,0:T(8,128)(2,1)} %get-tuple-element.54), channel_id=1, source_target_pairs={{16,32},{48,64},{80,96},{112,128},{144,160},{176,192},{208,224},{3... | collective-permute-start | bytes 417800 | tf_op jit(solution)/shard_map/ppermute | solution.py:371
  9.8 8.7 %collective-permute-start.1 = (bf16[544,128]{1,0:T(8,128)(2,1)}, bf16[544,128]{1,0:T(8,128)(2,1)S(1)}, u32[]{:S(2)}, u32[]{:S(2)}) collective-permute-start(bf16[544,128]{1,0:T(8,128)(2,1)} %get-tuple-element.55), channel_id=1, source_target_pairs={{0,16},{32,48},{64,80},{96,112},{128,144},{160,176},{192,208},{224... | collective-permute-start | bytes 417800 | tf_op jit(solution)/shard_map/ppermute | solution.py:371
  9.9 8.6 %collective-permute-start.2 = (f32[48,768]{1,0:T(8,128)}, f32[48,768]{1,0:T(8,128)S(1)}, u32[]{:S(2)}, u32[]{:S(2)}) collective-permute-start(f32[48,768]{1,0:T(8,128)} %get-tuple-element.56), channel_id=1, source_target_pairs={{0,2},{4,6},{8,10},{12,14},{2,0},{6,4},{10,8},{14,12},{1,3},{5,7},... | collective-permute-start | bytes 442376 | tf_op jit(solution)/shard_map/ppermute | solution.py:371
  10.0 8.5 %collective-permute-start.3 = (f32[48,768]{1,0:T(8,128)}, f32[48,768]{1,0:T(8,128)S(1)}, u32[]{:S(2)}, u32[]{:S(2)}) collective-permute-start(f32[48,768]{1,0:T(8,128)} %get-tuple-element.57), channel_id=1, source_target_pairs={{2,4},{6,8},{10,12},{4,2},{8,6},{12,10},{3,5},{7,9},{11,13},{5,3},... | collective-permute-start | bytes 442376 | tf_op jit(solution)/shard_map/ppermute | solution.py:371
  12.9 1.0 %copy-start.1 = (bf16[256,1024]{1,0:T(8,128)(2,1)S(1)}, bf16[256,1024]{1,0:T(8,128)(2,1)}, u32[]{:S(2)}) copy-start(bf16[256,1024]{1,0:T(8,128)(2,1)} %get-tuple-element.47.s0) | copy-start | bytes 1572868
  13.9 0.8 %copy-start.4 = (f32[128,128]{1,0:T(8,128)S(1)}, f32[128,128]{1,0:T(8,128)}, u32[]{:S(2)}) copy-start(f32[128,128]{1,0:T(8,128)} %get-tuple-element.48.weights) | copy-start | bytes 196612
  14.7 3.8 %copy-start = (f32[256,1024]{1,0:T(8,128)S(1)}, f32[256,1024]{1,0:T(8,128)}, u32[]{:S(2)}) copy-start(f32[256,1024]{1,0:T(8,128)} %get-tuple-element.52.v0) | copy-start | bytes 3145732
  14.7 3.8 %copy-start.2 = (bf16[256,1024]{1,0:T(8,128)(2,1)S(1)}, bf16[256,1024]{1,0:T(8,128)(2,1)}, u32[]{:S(2)}) copy-start(bf16[256,1024]{1,0:T(8,128)(2,1)} %get-tuple-element.47.s0) | copy-start | bytes 1572868
  14.7 3.8 %copy-start.3 = (f32[512,128]{1,0:T(8,128)S(1)}, f32[512,128]{1,0:T(8,128)}, u32[]{:S(2)}) copy-start(f32[512,128]{1,0:T(8,128)} %get-tuple-element.53.speeds) | copy-start | bytes 786436
  14.7 3.8 %copy-start.5 = (f32[128,128]{1,0:T(8,128)S(1)}, f32[128,128]{1,0:T(8,128)}, u32[]{:S(2)}) copy-start(f32[128,128]{1,0:T(8,128)} %get-tuple-element.48.weights) | copy-start | bytes 196612
  34.4 1.2 %collective-permute-start.4 = (f32[64,128]{1,0:T(8,128)S(1)}, f32[64,128]{1,0:T(8,128)S(1)}, u32[]{:S(2)}, u32[]{:S(2)}) collective-permute-start(f32[64,128]{1,0:T(8,128)S(1)} %get-tuple-element.63), channel_id=1, source_target_pairs={{0,2},{2,0},{1,3},{3,1},{4,6},{6,4},{5,7},{7,5},{8,10},{10,8},{9,1... | collective-permute-start | bytes 98312 | tf_op jit(solution)/shard_map/ppermute | solution.py:371
  35.6 3.9 %collective-permute-start.6 = (f32[64,128]{1,0:T(8,128)S(1)}, f32[64,128]{1,0:T(8,128)S(1)}, u32[]{:S(2)}, u32[]{:S(2)}) collective-permute-start(f32[64,128]{1,0:T(8,128)S(1)} %add.21), channel_id=1, source_target_pairs={{0,4},{8,12},{4,0},{12,8},{1,5},{9,13},{5,1},{13,9},{2,6},{10,14},... | collective-permute-start | bytes 98312 | tf_op jit(solution)/shard_map/ppermute | solution.py:371
  36.5 5.0 %collective-permute-start.5 = (f32[8,256]{1,0:T(8,128)S(1)}, f32[8,256]{1,0:T(8,128)S(1)}, u32[]{:S(2)}, u32[]{:S(2)}) collective-permute-start(f32[8,256]{1,0:T(8,128)S(1)} %get-tuple-element.64), channel_id=1, source_target_pairs={{2,4},{6,8},{10,12},{4,2},{8,6},{12,10},{3,5},{7,9},{11,13},{5,3},... | collective-permute-start | bytes 24584 | tf_op jit(solution)/shard_map/ppermute | solution.py:371
  41.4 5.1 %collective-permute-start.8 = (f32[64,128]{1,0:T(8,128)S(1)}, f32[64,128]{1,0:T(8,128)S(1)}, u32[]{:S(2)}, u32[]{:S(2)}) collective-permute-start(f32[64,128]{1,0:T(8,128)S(1)} %add.22), channel_id=1, source_target_pairs={{0,12},{4,8},{12,0},{8,4},{1,13},{5,9},{13,1},{9,5},{2,14},{6,10},... | collective-permute-start | bytes 98312 | tf_op jit(solution)/shard_map/ppermute | solution.py:371
  41.4 5.1 %collective-permute-start.7 = (f32[8,256]{1,0:T(8,128)S(1)}, f32[8,256]{1,0:T(8,128)S(1)}, u32[]{:S(2)}, u32[]{:S(2)}) collective-permute-start(f32[8,256]{1,0:T(8,128)S(1)} %get-tuple-element.67), channel_id=1, source_target_pairs={{0,2},{4,6},{8,10},{12,14},{2,0},{6,4},{10,8},{14,12},{1,3},{5,7},... | collective-permute-start | bytes 24584 | tf_op jit(solution)/shard_map/ppermute | solution.py:371
  46.5 5.7 %collective-permute-start.9 = (bf16[256,128]{1,0:T(8,128)(2,1)S(1)}, bf16[256,128]{1,0:T(8,128)(2,1)S(1)}, u32[]{:S(2)}, u32[]{:S(2)}) collective-permute-start(bf16[256,128]{1,0:T(8,128)(2,1)S(1)} %get-tuple-element.70), channel_id=1, source_target_pairs={{0,16},{32,48},{64,80},{96,112},{128,144},{160,176},{192,208},{224... | collective-permute-start | bytes 196616 | tf_op jit(solution)/shard_map/ppermute | solution.py:371
  48.4 3.9 %collective-permute-start.10 = (f32[64,128]{1,0:T(8,128)S(1)}, f32[64,128]{1,0:T(8,128)S(1)}, u32[]{:S(2)}, u32[]{:S(2)}) collective-permute-start(f32[64,128]{1,0:T(8,128)S(1)} %add.23), channel_id=1, source_target_pairs={{0,16},{32,48},{16,0},{48,32},{1,17},{33,49},{17,1},{49,33},{2,18}... | collective-permute-start | bytes 98312 | tf_op jit(solution)/shard_map/ppermute | solution.py:371
  52.3 9.5 %collective-permute-start.11 = (bf16[256,128]{1,0:T(8,128)(2,1)S(1)}, bf16[256,128]{1,0:T(8,128)(2,1)S(1)}, u32[]{:S(2)}, u32[]{:S(2)}) collective-permute-start(bf16[256,128]{1,0:T(8,128)(2,1)S(1)} %get-tuple-element.75), channel_id=1, source_target_pairs={{16,32},{48,64},{80,96},{112,128},{144,160},{176,192},{208,224},{3... | collective-permute-start | bytes 196616 | tf_op jit(solution)/shard_map/ppermute | solution.py:371
  56.3 5.5 %collective-permute-start.12 = (f32[64,128]{1,0:T(8,128)S(1)}, f32[64,128]{1,0:T(8,128)S(1)}, u32[]{:S(2)}, u32[]{:S(2)}) collective-permute-start(f32[64,128]{1,0:T(8,128)S(1)} %add.24), channel_id=1, source_target_pairs={{0,48},{16,32},{48,0},{32,16},{1,49},{17,33},{49,1},{33,17},{2,50}... | collective-permute-start | bytes 98312 | tf_op jit(solution)/shard_map/ppermute | solution.py:371
  61.8 4.0 %collective-permute-start.13 = (f32[64,128]{1,0:T(8,128)S(1)}, f32[64,128]{1,0:T(8,128)S(1)}, u32[]{:S(2)}, u32[]{:S(2)}) collective-permute-start(f32[64,128]{1,0:T(8,128)S(1)} %add.25), channel_id=1, source_target_pairs={{0,1},{64,65},{128,129},{192,193},{1,0},{65,64},{129,128},{193,192... | collective-permute-start | bytes 98312 | tf_op jit(solution)/shard_map/ppermute | solution.py:371
  65.8 5.1 %collective-permute-start.14 = (f32[64,128]{1,0:T(8,128)S(1)}, f32[64,128]{1,0:T(8,128)S(1)}, u32[]{:S(2)}, u32[]{:S(2)}) collective-permute-start(f32[64,128]{1,0:T(8,128)S(1)} %add.26), channel_id=1, source_target_pairs={{1,64},{65,128},{129,192},{193,0},{64,1},{128,65},{192,129},{0,193... | collective-permute-start | bytes 98312 | tf_op jit(solution)/shard_map/ppermute | solution.py:371
  71.0 9.2 %collective-permute-start.15 = (f32[64,128]{1,0:T(8,128)S(1)}, f32[64,128]{1,0:T(8,128)S(1)}, u32[]{:S(2)}, u32[]{:S(2)}) collective-permute-start(f32[64,128]{1,0:T(8,128)S(1)} %add.27.refs_0_), channel_id=1, source_target_pairs={{0,65},{1,192},{64,129},{128,193},{65,0},{192,1},{129,64},{193,128... | collective-permute-start | bytes 98312 | tf_op jit(solution)/shard_map/ppermute | solution.py:371

commit v2 on v1

--- a/solution.py
+++ b/solution.py
@@ -12,6 +12,7 @@
 NT = (((1,), (1,)), ((), ()))
 TN = (((0,), (0,)), ((), ()))
 PLANES = 4
+TAIL = 5
 PACK = 56
 
 
@@ -37,9 +38,9 @@
 def pack_kernel(
     cot_far, mom_far, sx_far, fx_far, sy_far, fy_far,
     w_in_far, b_in_far, w_mid_far, b_mid_far, w_out_far, b_out_far,
-    s0, v0, speeds, weights, x_even, x_odd, y_even, y_odd,
+    s0, v0, speeds, x_even, x_odd, y_even, y_odd,
     cot, mom, sx, fx, sy, fy, w_in, b_in, w_mid, b_mid, w_out, b_out,
-    mom_wide, x_ends, y_ends, sems,
+    mom_wide, x_ends, y_ends, weights, sems,
 ):
     copies = [
         pltpu.make_async_copy(far, near, sems.at[i])
@@ -65,6 +66,12 @@
     weights[96:97, 0:64] = b_in[...]
     weights[104:105, 0:64] = b_mid[...]
     weights[112:113, 0:16] = b_out[...]
+    rest = weights[...]
+    for term in range(3):
+        piece = rest.astype(bf16)
+        rest = rest - piece.astype(f32)
+        for i in range(8):
+            s0[256 + term * 16 : 272 + term * 16, i * 128 : i * 128 + 128] = piece[i * 16 : i * 16 + 16]
     copies[0].wait()
 
     def plane(z, carry):
@@ -86,7 +93,7 @@
     x_ends[0, 528:544, :] = speeds[pl.ds(128 + 7, 16, stride=8), :].astype(bf16)
     x_ends[1, 512:544, :] = jnp.zeros((32, 128), bf16)
     pick = edge_picker(8, 1024)
-    ends = mm(pick, s0[...], NT)
+    ends = mm(pick, s0[0:256, :], NT)
     ends_cot = mm(pick, v0[...].astype(bf16), NT)
     for side in (0, 1):
         y_ends[side, :, 0:256] = ends[side * 8 : side * 8 + 8]
@@ -106,8 +113,8 @@
     return lax.rem(lax.axis_index("y"), 2), lax.axis_index("c")
 
 
-def forward_kernel(s0, weights, ones_all, twos_all, base):
-    w_in, b_in, w_mid, b_mid, w_out, b_out = unbundled(weights)
+def forward_kernel(s0, ones_all, twos_all, base, weights):
+    w_in, b_in, w_mid, b_mid, w_out, b_out = unbundled(s0, weights)
     in_high, in_low = split(w_in[...])
     in_high, in_low = in_high.astype(f32), in_low.astype(f32)
     go_in = turned(jnp.concatenate([in_high, in_low, bias_rows(b_in[...])], 0))
@@ -131,7 +138,12 @@
     lax.fori_loop(0, 16 // PLANES, group, 0)
 
 
-def unbundled(weights):
+def unbundled(cells, weights):
+    for i in range(8):
+        first, second, third = (
+            cells[256 + term * 16 : 272 + term * 16, i * 128 : i * 128 + 128].astype(f32) for term in range(3)
+        )
+        weights[i * 16 : i * 16 + 16, :] = first + second + third
     return (
         weights.at[64:80, 0:64], weights.at[96:97, 0:64], weights.at[0:64, 0:64],
         weights.at[104:105, 0:64], weights.at[80:96, 0:64], weights.at[112:113, 0:16],
@@ -145,6 +157,35 @@
 def cat(items):
     return jnp.concatenate(items, 0)
 
+
+def stencil(coefs, tiles, before, after, ends, z, first):
+    end_lane = iota((16, 128), 1)
+    around = [before] + tiles + [after]
+    results = []
+    for x in range(8):
+        c = [
+            coefs[pl.ds(k * 128 + z * 8 + x, 1), :] for k in (0, first, first + 1, first + 2, first + 3)
+        ]
+        here = around[x + 1]
+        value = c[0] * here
+        if around[x + 2] is not None:
+            value = value - c[1] * around[x + 2]
+        if around[x] is not None:
+            value = value - c[2] * around[x]
+        right, left = pltpu.roll(here, 127, 1), pltpu.roll(here, 1, 1)
+        if ends is None:
+            end = 0.0
+        else:
+            end = ends[x]
+        right = jnp.where(end_lane == 127, end, right)
+        left = jnp.where(end_lane == 0, end, left)
+        value = value - c[3] * right - c[4] * left
+        results.append(value)
+    return results
+
+
+def tiles_of(value):
+    return [value[:, x * 128 : x * 128 + 128] for x in range(8)]
 
 def stacked(matrix):
     high, low = split(matrix)
@@ -171,11 +212,10 @@
 
 def main_kernel(
     ones_all, twos_all, base, s0, v0, speeds, x_odd, x_even, y_even, y_odd,
-    weights,
-    part, edge_coefs, x_even_out, x_odd_out, y_even_out, y_odd_out, sums,
-    coefs, moment_ends, cot_ends, v1_held, total, x_got, y_got, x_ends, y_ends,
+    v1, coefs, ones_grad_high, ones_grad_low, x_even_out, x_odd_out, y_even_out, y_odd_out, sums,
+    moment_ends, cot_ends, v1_held, total, x_got, y_got, x_ends, y_ends, weights,
 ):
-    w_in, b_in, w_mid, b_mid, w_out, _ = unbundled(weights)
+    w_in, b_in, w_mid, b_mid, w_out, _ = unbundled(s0, weights)
     odd_x, odd_y = parities()
     x_got[1 - odd_x] = x_even[...]
     x_got[odd_x] = x_odd[...]
@@ -205,8 +245,6 @@
         (keep, pull_x, pushed_x, pull_y, pushed_y, push_x, pulled_x, push_y, pulled_y)
     ):
         coefs[index * 128 : index * 128 + 128, :] = item
-    for index, item in enumerate((push_x, pulled_x, push_y, pulled_y)):
-        edge_coefs[index * 128 : index * 128 + 128, :] = item
 
     pick = edge_picker(8, 1024)
     ends = jnp.concatenate([y_next[:, 0:512], y_prev[:, 0:512]], 0).astype(bf16)
@@ -222,34 +260,6 @@
     ones = jnp.full((16, PLANES * 1024), 1.0, bf16)
     zeros = jnp.zeros((16, PLANES * 1024), bf16)
     total[...] = jnp.zeros_like(total)
-    end_lane = iota((16, 128), 1)
-
-    def stencil(tiles, before, after, ends, z, first):
-        around = [before] + tiles + [after]
-        results = []
-        for x in range(8):
-            c = [
-                coefs[pl.ds(k * 128 + z * 8 + x, 1), :] for k in (0, first, first + 1, first + 2, first + 3)
-            ]
-            here = around[x + 1]
-            value = c[0] * here
-            if around[x + 2] is not None:
-                value = value - c[1] * around[x + 2]
-            if around[x] is not None:
-                value = value - c[2] * around[x]
-            right, left = pltpu.roll(here, 127, 1), pltpu.roll(here, 1, 1)
-            if ends is None:
-                end = 0.0
-            else:
-                end = ends[x]
-            right = jnp.where(end_lane == 127, end, right)
-            left = jnp.where(end_lane == 0, end, left)
-            value = value - c[3] * right - c[4] * left
-            results.append(value)
-        return results
-
-    def tiles_of(value):
-        return [value[:, x * 128 : x * 128 + 128] for x in range(8)]
 
     def layers(inputs):
         one = jnp.tanh(mm(go_in, cat(inputs)))
@@ -263,14 +273,13 @@
         two_grad_pair = split(grad_two)
         grad_one = mm(back_mid, cat(three(two_grad_pair))) * (1.0 - one * one)
         one_grad_pair = split(grad_one)
-        grad_cells = mm(back_in, cat(three(one_grad_pair)))
         left_high = cat([state_pair[0], one_pair[0], adjoint_pair[0], ones])
         left_low = cat([state_pair[1], one_pair[1], adjoint_pair[1], zeros])
         right_high = cat([two_grad_pair[0], one_grad_pair[0], two_pair[0], ones])
         right_low = cat([two_grad_pair[1], one_grad_pair[1], two_pair[1], zeros])
         both = mm(cat([left_high, left_low]), right_high, NT)
         total[:, 0:208] += both[0:112] + both[112:224] + mm(left_high, right_low, NT)
-        return grad_cells
+        return one_grad_pair
 
     def group(index, carry):
         planes = [index * PLANES + i for i in range(PLANES)]
@@ -281,11 +290,8 @@
             results = []
             for i, z in enumerate(planes):
                 tiles = tiles_of(value[:, i * 1024 : i * 1024 + 1024])
-                if ends is None:
-                    results += stencil(tiles, None, None, None, z, first)
-                else:
-                    before, after = (ref[edges[i], :].astype(f32) for ref in (x_prev, x_next))
-                    results += stencil(tiles, before, after, tiles_of(ends[rows[i], :]), z, first)
+                before, after = (ref[edges[i], :].astype(f32) for ref in (x_prev, x_next))
+                results += stencil(coefs, tiles, before, after, tiles_of(ends[rows[i], :]), z, first)
             return join(results)
 
         state_zero = join([s0[r, :] for r in rows])
@@ -294,19 +300,19 @@
         adjoint = join([v0[r, :] for r in rows])
         state_pair = split(state_one)
         saved = layers(three(state_pair) + [ones])
-        grad_cells = backward(state_pair, *saved, adjoint)
+        grad_cells = mm(back_in, cat(three(backward(state_pair, *saved, adjoint))))
         adjoint = adjoint + grad_cells - moves(adjoint, cot_ends, rows_cot, 5)
         for i, r in enumerate(rows):
             tile = adjoint[:, i * 1024 : i * 1024 + 1024]
             v1_held[r, :] = tile.astype(bf16)
+            v1[r, :] = tile
             x_ends[0, r, :] = tile[:, 896:1024].astype(bf16)
             x_ends[1, r, :] = tile[:, 0:128].astype(bf16)
         lanes = pl.ds(pl.multiple_of(index * PLANES * 1024, PLANES * 1024), PLANES * 1024)
         one, two = ones_all[:, lanes], twos_all[:, lanes]
-        grad_cells = backward((state_zero, zeros), one, split(one), two, split(two), adjoint)
-        result = adjoint + grad_cells - moves(adjoint, None, None, 5)
-        for i, r in enumerate(rows):
-            part[r, :] = result[:, i * 1024 : i * 1024 + 1024]
+        grad_pair = backward((state_zero, zeros), one, split(one), two, split(two), adjoint)
+        ones_grad_high[:, lanes] = grad_pair[0]
+        ones_grad_low[:, lanes] = grad_pair[1]
         return carry
 
     lax.fori_loop(0, 16 // PLANES, group, 0)
@@ -326,7 +332,25 @@
     sums[...] = jnp.where(iota((64, 128), 1) < 64, first[16:80], rest)
 
 
-def finish_kernel(part, edge_coefs, x_even, x_odd, y_even, y_odd, out, ends_held, x_got, y_got):
+def tail_kernel(v1, coefs, grad_high, grad_low, s0, part, weights):
+    back_in = turned(stacked(unbundled(s0, weights)[0][...].T))
+
+    def group(index, carry):
+        lanes = pl.ds(pl.multiple_of(index * PLANES * 1024, PLANES * 1024), PLANES * 1024)
+        high, low = grad_high[:, lanes], grad_low[:, lanes]
+        grad_cells = mm(back_in, cat([high, low, high]))
+        for i in range(PLANES):
+            z = index * PLANES + i
+            rows = pl.ds(pl.multiple_of(z * 16, 16), 16)
+            here = v1[rows, :]
+            moved = stencil(coefs, tiles_of(here), None, None, None, z, 5)
+            part[rows, :] = here + grad_cells[:, i * 1024 : i * 1024 + 1024] - join(moved)
+        return carry
+
+    lax.fori_loop(0, 16 // PLANES, group, 0)
+
+
+def finish_kernel(part, coefs, x_even, x_odd, y_even, y_odd, out, ends_held, x_got, y_got):
     odd_x, odd_y = parities()
     x_got[1 - odd_x] = x_even[...]
     x_got[odd_x] = x_odd[...]
@@ -342,7 +366,7 @@
         start = pl.multiple_of(z * 16, 16)
         rows = pl.ds(start, 16)
         for x in range(8):
-            c = [edge_coefs[pl.ds(k * 128 + z * 8 + x, 1), :] for k in range(4)]
+            c = [coefs[pl.ds(k * 128 + z * 8 + x, 1), :] for k in (5, 6, 7, 8)]
             value = part[rows, x * 128 : x * 128 + 128]
             weight = jnp.where(end_lane == 127, c[2], jnp.where(end_lane == 0, c[3], 0.0))
             value = value + weight * ends_held[rows, x * 128 : x * 128 + 128]
@@ -400,12 +424,12 @@
         sx, fx, sy, fy = (item.reshape(128, 128) for item in (speed_x, flag_x, speed_y, flag_y))
         b_in, b_mid, b_out = b_in.reshape(1, 64), b_mid.reshape(1, 64), b_out.reshape(1, 16)
         w_out = w_out.T
-        s0, v0, speeds, bundle, x_even, x_odd, y_even, y_odd = pl.pallas_call(
+        s0, v0, speeds, x_even, x_odd, y_even, y_odd = pl.pallas_call(
             pack_kernel,
             in_specs=[far] * 12,
             out_shape=(
-                shape((256, 1024), bf16), shape((256, 1024), f32), shape((512, 128), f32),
-                shape((128, 128), f32), shape((544, 128), bf16), shape((544, 128), bf16),
+                shape((304, 1024), bf16), shape((256, 1024), f32), shape((512, 128), f32),
+                shape((544, 128), bf16), shape((544, 128), bf16),
                 shape((48, 768), f32), shape((48, 768), f32),
             ),
             scratch_shapes=[
@@ -415,7 +439,7 @@
                 pltpu.VMEM((16, 64), f32), pltpu.VMEM((1, 64), f32), pltpu.VMEM((64, 64), f32),
                 pltpu.VMEM((1, 64), f32), pltpu.VMEM((16, 64), f32), pltpu.VMEM((1, 16), f32),
                 pltpu.VMEM((2048, 128), f32), pltpu.VMEM((2, 544, 128), bf16),
-                pltpu.VMEM((2, 8, 768), f32), pltpu.SemaphoreType.DMA((12,)),
+                pltpu.VMEM((2, 8, 768), f32), pltpu.VMEM((128, 128), f32), pltpu.SemaphoreType.DMA((12,)),
             ],
             compiler_params=params(PACK),
             name="pack",
@@ -425,29 +449,31 @@
         ones_all, twos_all, base = pl.pallas_call(
             forward_kernel,
             out_shape=(shape((64, 16384), f32), shape((64, 16384), f32), shape((256, 1024), f32)),
+            scratch_shapes=[pltpu.VMEM((128, 128), f32)],
             compiler_params=params(24),
             cost_estimate=cost(5000000000, 16000000),
             name="forward",
-        )(s0, bundle)
-        part, edge_coefs, x_even, x_odd, y_even, y_odd, sums = pl.pallas_call(
+        )(s0)
+        v1, coefs, grad_high, grad_low, x_even, x_odd, y_even, y_odd, sums = pl.pallas_call(
             main_kernel,
             out_shape=(
-                shape((256, 1024), f32), shape((512, 128), f32),
+                shape((256, 1024), f32), shape((9 * 128, 128), f32),
+                shape((64, 16384), bf16), shape((64, 16384), bf16),
                 shape((256, 128), bf16), shape((256, 128), bf16),
                 shape((8, 256), f32), shape((8, 256), f32), shape((64, 128), f32),
             ),
             scratch_shapes=[
-                pltpu.VMEM((9 * 128, 128), f32), pltpu.VMEM((256, 1024), f32),
+                pltpu.VMEM((256, 1024), f32),
                 pltpu.VMEM((256, 1024), f32), pltpu.VMEM((256, 1024), bf16),
                 pltpu.VMEM((112, 256), f32), pltpu.VMEM((2, 544, 128), bf16),
                 pltpu.VMEM((2, 8, 768), f32), pltpu.VMEM((2, 256, 128), bf16),
-                pltpu.VMEM((2, 8, 256), f32),
+                pltpu.VMEM((2, 8, 256), f32), pltpu.VMEM((128, 128), f32),
             ],
             compiler_params=params(32),
             cost_estimate=cost(15000000000, 40000000),
             name="network",
         )(
-            ones_all, twos_all, base, s0, v0, speeds, x_odd, x_even, y_even, y_odd, bundle
+            ones_all, twos_all, base, s0, v0, speeds, x_odd, x_even, y_even, y_odd
         )
         steps = (
             ("c", [(0, 1)]),
@@ -472,7 +498,19 @@
                 along, value, route = places[name]
                 value, sums = lax.optimization_barrier((value, sums))
                 moving[name] = pairs(value, along, route)
+            if index == TAIL:
+                v1, sums = lax.optimization_barrier((v1, sums))
+                part = pl.pallas_call(
+                    tail_kernel,
+                    out_shape=shape((256, 1024), f32),
+                    scratch_shapes=[pltpu.VMEM((128, 128), f32)],
+                    compiler_params=params(16),
+                    cost_estimate=cost(2000000000, 8000000),
+                    name="tail",
+                )(v1, coefs, grad_high, grad_low, s0)
             sums = sums + pairs(sums, axis, links)
+            if index == TAIL:
+                part, sums = lax.optimization_barrier((part, sums))
             if moving:
                 names = list(moving)
                 *values, sums = lax.optimization_barrier(tuple(moving[n] for n in names) + (sums,))
@@ -488,7 +526,7 @@
             compiler_params=params(16),
             cost_estimate=cost(10000000, 6000000),
             name="finish",
-        )(part, edge_coefs, x_even, x_odd, y_even, y_odd)
+        )(part, coefs, x_even, x_odd, y_even, y_odd)
 
         d_in, d_b_in, d_mid, d_b_mid, d_out, d_b_out = pl.pallas_call(
             lambda *refs: weights_kernel(1.0 / cells, *refs),

time: 81.1 us -> 79.4 us (0.979)
  waiting for transfers between devices: 21.5 us -> 19.7 us
    ppermute x16, waiting for transfers between devices: 21.5 us -> 19.7 us  [pairs(): lax.ppermute(value, axis, [(a, b) for a, b in links] + [(b, a) for a, b i...]
    unnamed x12 -> x8, local copies, waits for them, and re-layouts: 1.89 us -> 1.08 us
    pallas_call x2 -> x3, Pallas kernels: 20.2 us -> 20.8 us  [the longest x1 15 us: local(): pl.pallas_call(main_kernel, out_shape=(shape((256, 1024), f32), shape((9...]
  transfers between devices with their start and end apart: 16 -> 16, of which waited for: 9 -> 9; matrix products, arithmetic and copies ran while one was open for 0% -> 0% of each run, Pallas kernels for 7% -> 9%
where the time goes in v2:
time: 79.4 us; the launch traced here: 78.6 us
  starting transfers between devices  29.7 us (37%)
  Pallas kernels  27.3 us (34%)
  waiting for transfers between devices  19.7 us (25%)
  local copies, waits for them, and re-layouts  1.08 us (1%)
    ppermute x16, starting transfers between devices, pairs(): lax.ppermute(value, axis, [(a, b) for a, b in links] + [(b, a) for a, b i...  29.7 us
    ppermute x16, waiting for transfers between devices, pairs(): lax.ppermute(value, axis, [(a, b) for a, b in links] + [(b, a) for a, b i...  19.7 us
    pallas_call x1, Pallas kernels, local(): pl.pallas_call(main_kernel, out_shape=(shape((256, 1024), f32), shape((9...  15 us
    pallas_call x1, Pallas kernels, local(): pl.pallas_call(pack_kernel, in_specs=[far] * 12, out_shape=(shape((304, 1...  4.34 us
    pallas_call x1, Pallas kernels, local(): pl.pallas_call(forward_kernel, out_shape=(shape((64, 16384), f32), shape(...  3.46 us
    pallas_call x1, Pallas kernels, local(): pl.pallas_call(finish_kernel, out_shape=shape((2048, 128), f32), scratch_...  2.32 us
  transfers between devices with their start and end apart: 16, of which 9 were waited for; matrix products, arithmetic and copies ran while one was open for 0% of the time, Pallas kernels for 9%

profile of v2, /device:TPU:30, one launch (start us, length us, event | category | flops | bytes accessed | tf_op | source)
XLA Modules:
  0.0 78.6 jit_solution(16091434613189104036)
XLA Ops:
  0.6 4.3 %pack.1 = (bf16[304,1024]{1,0:T(8,128)(2,1)}, f32[256,1024]{1,0:T(8,128)}, f32[512,128]{1,0:T(8,128)}, bf16[544,128]{1,0:T(8,128)(2,1)}, bf16[544,128]{1,0:T(8,1...) custom-call(f32[2048,128]{1,0:T(8,128)} %bitcast.15, bf16[2048,128]{1,0:T(8,128)(2,1)} %bitcast.17, ...), custom_call_target="tpu_custom_call" | custom-call | tf_op jit(solution)/shard_map/pack/pallas_call | solution.py:427
  5.0 4.8 %collective-permute-start = (bf16[544,128]{1,0:T(8,128)(2,1)}, bf16[544,128]{1,0:T(8,128)(2,1)S(1)}, u32[]{:S(2)}, u32[]{:S(2)}) collective-permute-start(bf16[544,128]{1,0:T(8,128)(2,1)} %get-tuple-element.58), channel_id=1, source_target_pairs={{16,32},{48,64},{80,96},{112,128},{144,160},{176,192},{208,224},{3... | collective-permute-start | bytes 417800 | tf_op jit(solution)/shard_map/ppermute | solution.py:395
  9.8 0.1 collective-permute-start.1
  9.9 0.1 collective-permute-start.2
  10.0 2.8 %collective-permute-start.3 = (f32[48,768]{1,0:T(8,128)}, f32[48,768]{1,0:T(8,128)S(1)}, u32[]{:S(2)}, u32[]{:S(2)}) collective-permute-start(f32[48,768]{1,0:T(8,128)} %get-tuple-element.61), channel_id=1, source_target_pairs={{2,4},{6,8},{10,12},{4,2},{8,6},{12,10},{3,5},{7,9},{11,13},{5,3},... | collective-permute-start | bytes 442376 | tf_op jit(solution)/shard_map/ppermute | solution.py:395
  12.9 0.0 copy-start
  12.9 1.1 %copy-done = bf16[304,1024]{1,0:T(8,128)(2,1)S(1)} copy-done((bf16[304,1024]{1,0:T(8,128)(2,1)S(1)}, bf16[304,1024]{1,0:T(8,128)(2,1)}, u32[]{:S(2)}) %copy-start) | copy-done | bytes 622616
  13.9 0.0 copy-start.1
  13.9 0.0 copy-start.2
  13.9 0.0 copy-start.3
  13.9 3.5 %forward.1 = (f32[64,16384]{1,0:T(8,128)S(1)}, f32[64,16384]{1,0:T(8,128)S(1)}, f32[256,1024]{1,0:T(8,128)S(1)}) custom-call(bf16[304,1024]{1,0:T(8,128)(2,1)S(1)} %copy-done), custom_call_target="tpu_custom_call" | custom-call | flops 5000000000 | bytes 16000000 | tf_op jit(solution)/shard_map/forward/pallas_call | solution.py:449
  17.4 1.1 %collective-permute-done.x_odd = bf16[544,128]{1,0:T(8,128)(2,1)S(1)} collective-permute-done((bf16[544,128]{1,0:T(8,128)(2,1)}, bf16[544,128]{1,0:T(8,128)(2,1)S(1)}, u32[]{:S(2)}, u32[]{:S(2)}) %collective-permute-start) | collective-permute-done | bytes 139296 | tf_op jit(solution)/shard_map/ppermute | solution.py:395
  18.5 0.0 collective-permute-done.1.x_even
  18.5 0.0 collective-permute-done.2.y_even
  18.5 0.0 collective-permute-done.3.y_odd
  18.5 0.0 copy-done.1
  18.5 0.0 copy-done.2
  18.5 0.0 copy-done.3
  18.5 15.0 %network.1 = (f32[256,1024]{1,0:T(8,128)S(1)}, f32[1152,128]{1,0:T(8,128)S(1)}, bf16[64,16384]{1,0:T(8,128)(2,1)S(1)}, bf16[64,16384]{1,0:T(8,128)(2,1)S(1)}, bf...) custom-call(f32[64,16384]{1,0:T(8,128)S(1)} %get-tuple-element.53.on, ...), custom_call_target="tpu_custom_call" | custom-call | flops 15000000512 | bytes 40000000 | tf_op jit(solution)/shard_map/network/pallas_call | solution.py:457
  33.6 0.0 collective-permute-start.4
  33.6 1.2 %collective-permute-done.4 = f32[64,128]{1,0:T(8,128)S(1)} collective-permute-done((f32[64,128]{1,0:T(8,128)S(1)}, f32[64,128]{1,0:T(8,128)S(1)}, u32[]{:S(2)}, u32[]{:S(2)}) %collective-permute-start.4) | collective-permute-done | bytes 32800 | tf_op jit(solution)/shard_map/ppermute | solution.py:395
  34.8 0.8 %collective-permute-start.6 = (f32[64,128]{1,0:T(8,128)S(1)}, f32[64,128]{1,0:T(8,128)S(1)}, u32[]{:S(2)}, u32[]{:S(2)}) collective-permute-start(f32[64,128]{1,0:T(8,128)S(1)} %add.21), channel_id=1, source_target_pairs={{0,4},{8,12},{4,0},{12,8},{1,5},{9,13},{5,1},{13,9},{2,6},{10,14},... | collective-permute-start | bytes 98312 | tf_op jit(solution)/shard_map/ppermute | solution.py:395
  35.6 2.6 %collective-permute-start.5 = (f32[8,256]{1,0:T(8,128)S(1)}, f32[8,256]{1,0:T(8,128)S(1)}, u32[]{:S(2)}, u32[]{:S(2)}) collective-permute-start(f32[8,256]{1,0:T(8,128)S(1)} %get-tuple-element.68), channel_id=1, source_target_pairs={{2,4},{6,8},{10,12},{4,2},{8,6},{12,10},{3,5},{7,9},{11,13},{5,3},... | collective-permute-start | bytes 24584 | tf_op jit(solution)/shard_map/ppermute | solution.py:395
  38.2 0.5 collective-permute-done.6
  38.8 1.9 %collective-permute-done.5.y_odd = f32[8,256]{1,0:T(8,128)S(1)} collective-permute-done((f32[8,256]{1,0:T(8,128)S(1)}, f32[8,256]{1,0:T(8,128)S(1)}, u32[]{:S(2)}, u32[]{:S(2)}) %collective-permute-start.5) | collective-permute-done | bytes 8224 | tf_op jit(solution)/shard_map/ppermute | solution.py:395
  40.6 0.0 collective-permute-start.8
  40.6 0.8 collective-permute-start.7
  41.4 4.4 %collective-permute-done.8 = f32[64,128]{1,0:T(8,128)S(1)} collective-permute-done((f32[64,128]{1,0:T(8,128)S(1)}, f32[64,128]{1,0:T(8,128)S(1)}, u32[]{:S(2)}, u32[]{:S(2)}) %collective-permute-start.8) | collective-permute-done | bytes 32800 | tf_op jit(solution)/shard_map/ppermute | solution.py:395
  45.7 0.0 collective-permute-done.7.y_even
  45.7 1.0 %collective-permute-start.9 = (bf16[256,128]{1,0:T(8,128)(2,1)S(1)}, bf16[256,128]{1,0:T(8,128)(2,1)S(1)}, u32[]{:S(2)}, u32[]{:S(2)}) collective-permute-start(bf16[256,128]{1,0:T(8,128)(2,1)S(1)} %get-tuple-element.74), channel_id=1, source_target_pairs={{0,16},{32,48},{64,80},{96,112},{128,144},{160,176},{192,208},{224... | collective-permute-start | bytes 196616 | tf_op jit(solution)/shard_map/ppermute | solution.py:395
  46.7 1.1 %collective-permute-start.10 = (f32[64,128]{1,0:T(8,128)S(1)}, f32[64,128]{1,0:T(8,128)S(1)}, u32[]{:S(2)}, u32[]{:S(2)}) collective-permute-start(f32[64,128]{1,0:T(8,128)S(1)} %add.23), channel_id=1, source_target_pairs={{0,16},{32,48},{16,0},{48,32},{1,17},{33,49},{17,1},{49,33},{2,18}... | collective-permute-start | bytes 98312 | tf_op jit(solution)/shard_map/ppermute | solution.py:395
  47.9 2.8 %collective-permute-done.10 = f32[64,128]{1,0:T(8,128)S(1)} collective-permute-done((f32[64,128]{1,0:T(8,128)S(1)}, f32[64,128]{1,0:T(8,128)S(1)}, u32[]{:S(2)}, u32[]{:S(2)}) %collective-permute-start.10) | collective-permute-done | bytes 32800 | tf_op jit(solution)/shard_map/ppermute | solution.py:395
  50.7 0.0 collective-permute-done.9.x_even
  50.7 4.0 %collective-permute-start.11 = (bf16[256,128]{1,0:T(8,128)(2,1)S(1)}, bf16[256,128]{1,0:T(8,128)(2,1)S(1)}, u32[]{:S(2)}, u32[]{:S(2)}) collective-permute-start(bf16[256,128]{1,0:T(8,128)(2,1)S(1)} %get-tuple-element.77), channel_id=1, source_target_pairs={{16,32},{48,64},{80,96},{112,128},{144,160},{176,192},{208,224},{3... | collective-permute-start | bytes 196616 | tf_op jit(solution)/shard_map/ppermute | solution.py:395
  54.7 0.1 collective-permute-start.12
  54.8 5.4 %collective-permute-done.12 = f32[64,128]{1,0:T(8,128)S(1)} collective-permute-done((f32[64,128]{1,0:T(8,128)S(1)}, f32[64,128]{1,0:T(8,128)S(1)}, u32[]{:S(2)}, u32[]{:S(2)}) %collective-permute-start.12) | collective-permute-done | bytes 32800 | tf_op jit(solution)/shard_map/ppermute | solution.py:395
  60.2 0.0 collective-permute-done.11.x_odd
  60.2 2.1 %collective-permute-start.13 = (f32[64,128]{1,0:T(8,128)S(1)}, f32[64,128]{1,0:T(8,128)S(1)}, u32[]{:S(2)}, u32[]{:S(2)}) collective-permute-start(f32[64,128]{1,0:T(8,128)S(1)} %add.25), channel_id=1, source_target_pairs={{0,1},{64,65},{128,129},{192,193},{1,0},{65,64},{129,128},{193,192... | collective-permute-start | bytes 98312 | tf_op jit(solution)/shard_map/ppermute | solution.py:395
  62.3 1.5 %tail.1.part = f32[256,1024]{1,0:T(8,128)S(1)} custom-call(f32[256,1024]{1,0:T(8,128)S(1)} %get-tuple-element.80.v1, f32[1152,128]{1,0:T(8,128)S(1)} %get-tuple-element.81.coefs, bf16[64,16384]{1,0:T(8,128)(2,1)S(1)} %get-tuple-element.82.grad_high, bf16[64,16384]{1,0:T(8,128)(2,1)S(1)} %get-tuple-element.83.grad_low, bf16[304,1024]{1,0:T(8,128)(2,1)S(1)} %copy-done.1), custom_call_target="tpu_custom_call" | custom-call | flops 2000000000 | bytes 8000000 | tf_op jit(solution)/shard_map/tail/pallas_call | solution.py:503
  63.8 0.4 collective-permute-done.13
  64.2 3.1 %collective-permute-start.14 = (f32[64,128]{1,0:T(8,128)S(1)}, f32[64,128]{1,0:T(8,128)S(1)}, u32[]{:S(2)}, u32[]{:S(2)}) collective-permute-start(f32[64,128]{1,0:T(8,128)S(1)} %add.26), channel_id=1, source_target_pairs={{1,64},{65,128},{129,192},{193,0},{64,1},{128,65},{192,129},{0,193... | collective-permute-start | bytes 98312 | tf_op jit(solution)/shard_map/ppermute | solution.py:395
  67.4 2.0 %collective-permute-done.14 = f32[64,128]{1,0:T(8,128)S(1)} collective-permute-done((f32[64,128]{1,0:T(8,128)S(1)}, f32[64,128]{1,0:T(8,128)S(1)}, u32[]{:S(2)}, u32[]{:S(2)}) %collective-permute-start.14) | collective-permute-done | bytes 32800 | tf_op jit(solution)/shard_map/ppermute | solution.py:395
  69.4 6.2 %collective-permute-start.15 = (f32[64,128]{1,0:T(8,128)S(1)}, f32[64,128]{1,0:T(8,128)S(1)}, u32[]{:S(2)}, u32[]{:S(2)}) collective-permute-start(f32[64,128]{1,0:T(8,128)S(1)} %add.27.refs_0_), channel_id=1, source_target_pairs={{0,65},{1,192},{64,129},{128,193},{65,0},{192,1},{129,64},{193,128... | collective-permute-start | bytes 98312 | tf_op jit(solution)/shard_map/ppermute | solution.py:395
  75.6 2.3 %finish.1 = f32[2048,128]{1,0:T(8,128)} custom-call(f32[256,1024]{1,0:T(8,128)S(1)} %tail.1.part, f32[1152,128]{1,0:T(8,128)S(1)} %get-tuple-element.81.coefs, bf16[256,128]{1,0:T(8,128)(2,1)S(1)} %collective-permute-done.9.x_even, bf16[256,128]{1,0:T(8,128)(2,1)S(1)} %collective-permute-done.11.x_odd, f32[8,256]{1,0:T(8,128)S(1)} %collective-permute-done.7.y_even, ...), custom_call_target="tpu_custom_call" | custom-call | flops 10000000 | bytes 6000000 | tf_op jit(solution)/shard_map/finish/pallas_call | solution.py:520
  77.9 0.0 collective-permute-done.15.refs_1_
  77.9 0.7 weights.1
  (7 shorter events, 0.0 us)
Async XLA Ops:
  5.0 13.5 %collective-permute-start = (bf16[544,128]{1,0:T(8,128)(2,1)}, bf16[544,128]{1,0:T(8,128)(2,1)S(1)}, u32[]{:S(2)}, u32[]{:S(2)}) collective-permute-start(bf16[544,128]{1,0:T(8,128)(2,1)} %get-tuple-element.58), channel_id=1, source_target_pairs={{16,32},{48,64},{80,96},{112,128},{144,160},{176,192},{208,224},{3... | collective-permute-start | bytes 417800 | tf_op jit(solution)/shard_map/ppermute | solution.py:395
  9.8 8.7 %collective-permute-start.1 = (bf16[544,128]{1,0:T(8,128)(2,1)}, bf16[544,128]{1,0:T(8,128)(2,1)S(1)}, u32[]{:S(2)}, u32[]{:S(2)}) collective-permute-start(bf16[544,128]{1,0:T(8,128)(2,1)} %get-tuple-element.59), channel_id=1, source_target_pairs={{0,16},{32,48},{64,80},{96,112},{128,144},{160,176},{192,208},{224... | collective-permute-start | bytes 417800 | tf_op jit(solution)/shard_map/ppermute | solution.py:395
  9.9 8.6 %collective-permute-start.2 = (f32[48,768]{1,0:T(8,128)}, f32[48,768]{1,0:T(8,128)S(1)}, u32[]{:S(2)}, u32[]{:S(2)}) collective-permute-start(f32[48,768]{1,0:T(8,128)} %get-tuple-element.60), channel_id=1, source_target_pairs={{0,2},{4,6},{8,10},{12,14},{2,0},{6,4},{10,8},{14,12},{1,3},{5,7},... | collective-permute-start | bytes 442376 | tf_op jit(solution)/shard_map/ppermute | solution.py:395
  10.0 8.5 %collective-permute-start.3 = (f32[48,768]{1,0:T(8,128)}, f32[48,768]{1,0:T(8,128)S(1)}, u32[]{:S(2)}, u32[]{:S(2)}) collective-permute-start(f32[48,768]{1,0:T(8,128)} %get-tuple-element.61), channel_id=1, source_target_pairs={{2,4},{6,8},{10,12},{4,2},{8,6},{12,10},{3,5},{7,9},{11,13},{5,3},... | collective-permute-start | bytes 442376 | tf_op jit(solution)/shard_map/ppermute | solution.py:395
  12.9 1.1 %copy-start = (bf16[304,1024]{1,0:T(8,128)(2,1)S(1)}, bf16[304,1024]{1,0:T(8,128)(2,1)}, u32[]{:S(2)}) copy-start(bf16[304,1024]{1,0:T(8,128)(2,1)} %get-tuple-element.52.s0) | copy-start | bytes 1867780
  13.9 4.6 %copy-start.1 = (bf16[304,1024]{1,0:T(8,128)(2,1)S(1)}, bf16[304,1024]{1,0:T(8,128)(2,1)}, u32[]{:S(2)}) copy-start(bf16[304,1024]{1,0:T(8,128)(2,1)} %get-tuple-element.52.s0) | copy-start | bytes 1867780
  13.9 4.6 %copy-start.2 = (f32[256,1024]{1,0:T(8,128)S(1)}, f32[256,1024]{1,0:T(8,128)}, u32[]{:S(2)}) copy-start(f32[256,1024]{1,0:T(8,128)} %get-tuple-element.56.v0) | copy-start | bytes 3145732
  13.9 4.6 %copy-start.3 = (f32[512,128]{1,0:T(8,128)S(1)}, f32[512,128]{1,0:T(8,128)}, u32[]{:S(2)}) copy-start(f32[512,128]{1,0:T(8,128)} %get-tuple-element.57.speeds) | copy-start | bytes 786436
  33.6 1.2 %collective-permute-start.4 = (f32[64,128]{1,0:T(8,128)S(1)}, f32[64,128]{1,0:T(8,128)S(1)}, u32[]{:S(2)}, u32[]{:S(2)}) collective-permute-start(f32[64,128]{1,0:T(8,128)S(1)} %get-tuple-element.67), channel_id=1, source_target_pairs={{0,2},{2,0},{1,3},{3,1},{4,6},{6,4},{5,7},{7,5},{8,10},{10,8},{9,1... | collective-permute-start | bytes 98312 | tf_op jit(solution)/shard_map/ppermute | solution.py:395
  34.8 3.9 %collective-permute-start.6 = (f32[64,128]{1,0:T(8,128)S(1)}, f32[64,128]{1,0:T(8,128)S(1)}, u32[]{:S(2)}, u32[]{:S(2)}) collective-permute-start(f32[64,128]{1,0:T(8,128)S(1)} %add.21), channel_id=1, source_target_pairs={{0,4},{8,12},{4,0},{12,8},{1,5},{9,13},{5,1},{13,9},{2,6},{10,14},... | collective-permute-start | bytes 98312 | tf_op jit(solution)/shard_map/ppermute | solution.py:395
  35.6 5.0 %collective-permute-start.5 = (f32[8,256]{1,0:T(8,128)S(1)}, f32[8,256]{1,0:T(8,128)S(1)}, u32[]{:S(2)}, u32[]{:S(2)}) collective-permute-start(f32[8,256]{1,0:T(8,128)S(1)} %get-tuple-element.68), channel_id=1, source_target_pairs={{2,4},{6,8},{10,12},{4,2},{8,6},{12,10},{3,5},{7,9},{11,13},{5,3},... | collective-permute-start | bytes 24584 | tf_op jit(solution)/shard_map/ppermute | solution.py:395
  40.6 5.1 %collective-permute-start.8 = (f32[64,128]{1,0:T(8,128)S(1)}, f32[64,128]{1,0:T(8,128)S(1)}, u32[]{:S(2)}, u32[]{:S(2)}) collective-permute-start(f32[64,128]{1,0:T(8,128)S(1)} %add.22), channel_id=1, source_target_pairs={{0,12},{4,8},{12,0},{8,4},{1,13},{5,9},{13,1},{9,5},{2,14},{6,10},... | collective-permute-start | bytes 98312 | tf_op jit(solution)/shard_map/ppermute | solution.py:395
  40.6 5.1 %collective-permute-start.7 = (f32[8,256]{1,0:T(8,128)S(1)}, f32[8,256]{1,0:T(8,128)S(1)}, u32[]{:S(2)}, u32[]{:S(2)}) collective-permute-start(f32[8,256]{1,0:T(8,128)S(1)} %get-tuple-element.71), channel_id=1, source_target_pairs={{0,2},{4,6},{8,10},{12,14},{2,0},{6,4},{10,8},{14,12},{1,3},{5,7},... | collective-permute-start | bytes 24584 | tf_op jit(solution)/shard_map/ppermute | solution.py:395
  45.7 4.9 %collective-permute-start.9 = (bf16[256,128]{1,0:T(8,128)(2,1)S(1)}, bf16[256,128]{1,0:T(8,128)(2,1)S(1)}, u32[]{:S(2)}, u32[]{:S(2)}) collective-permute-start(bf16[256,128]{1,0:T(8,128)(2,1)S(1)} %get-tuple-element.74), channel_id=1, source_target_pairs={{0,16},{32,48},{64,80},{96,112},{128,144},{160,176},{192,208},{224... | collective-permute-start | bytes 196616 | tf_op jit(solution)/shard_map/ppermute | solution.py:395
  46.7 3.9 %collective-permute-start.10 = (f32[64,128]{1,0:T(8,128)S(1)}, f32[64,128]{1,0:T(8,128)S(1)}, u32[]{:S(2)}, u32[]{:S(2)}) collective-permute-start(f32[64,128]{1,0:T(8,128)S(1)} %add.23), channel_id=1, source_target_pairs={{0,16},{32,48},{16,0},{48,32},{1,17},{33,49},{17,1},{49,33},{2,18}... | collective-permute-start | bytes 98312 | tf_op jit(solution)/shard_map/ppermute | solution.py:395
  50.7 9.5 %collective-permute-start.11 = (bf16[256,128]{1,0:T(8,128)(2,1)S(1)}, bf16[256,128]{1,0:T(8,128)(2,1)S(1)}, u32[]{:S(2)}, u32[]{:S(2)}) collective-permute-start(bf16[256,128]{1,0:T(8,128)(2,1)S(1)} %get-tuple-element.77), channel_id=1, source_target_pairs={{16,32},{48,64},{80,96},{112,128},{144,160},{176,192},{208,224},{3... | collective-permute-start | bytes 196616 | tf_op jit(solution)/shard_map/ppermute | solution.py:395
  54.7 5.5 %collective-permute-start.12 = (f32[64,128]{1,0:T(8,128)S(1)}, f32[64,128]{1,0:T(8,128)S(1)}, u32[]{:S(2)}, u32[]{:S(2)}) collective-permute-start(f32[64,128]{1,0:T(8,128)S(1)} %add.24), channel_id=1, source_target_pairs={{0,48},{16,32},{48,0},{32,16},{1,49},{17,33},{49,1},{33,17},{2,50}... | collective-permute-start | bytes 98312 | tf_op jit(solution)/shard_map/ppermute | solution.py:395
  60.2 4.0 %collective-permute-start.13 = (f32[64,128]{1,0:T(8,128)S(1)}, f32[64,128]{1,0:T(8,128)S(1)}, u32[]{:S(2)}, u32[]{:S(2)}) collective-permute-start(f32[64,128]{1,0:T(8,128)S(1)} %add.25), channel_id=1, source_target_pairs={{0,1},{64,65},{128,129},{192,193},{1,0},{65,64},{129,128},{193,192... | collective-permute-start | bytes 98312 | tf_op jit(solution)/shard_map/ppermute | solution.py:395
  64.2 5.1 %collective-permute-start.14 = (f32[64,128]{1,0:T(8,128)S(1)}, f32[64,128]{1,0:T(8,128)S(1)}, u32[]{:S(2)}, u32[]{:S(2)}) collective-permute-start(f32[64,128]{1,0:T(8,128)S(1)} %add.26), channel_id=1, source_target_pairs={{1,64},{65,128},{129,192},{193,0},{64,1},{128,65},{192,129},{0,193... | collective-permute-start | bytes 98312 | tf_op jit(solution)/shard_map/ppermute | solution.py:395
  69.4 8.5 %collective-permute-start.15 = (f32[64,128]{1,0:T(8,128)S(1)}, f32[64,128]{1,0:T(8,128)S(1)}, u32[]{:S(2)}, u32[]{:S(2)}) collective-permute-start(f32[64,128]{1,0:T(8,128)S(1)} %add.27.refs_0_), channel_id=1, source_target_pairs={{0,65},{1,192},{64,129},{128,193},{65,0},{192,1},{129,64},{193,128... | collective-permute-start | bytes 98312 | tf_op jit(solution)/shard_map/ppermute | solution.py:395

commit v3 on v2

--- a/solution.py
+++ b/solution.py
@@ -12,7 +12,7 @@
 NT = (((1,), (1,)), ((), ()))
 TN = (((0,), (0,)), ((), ()))
 PLANES = 4
-TAIL = 5
+TAIL = 3
 PACK = 56
 
 
@@ -212,7 +212,7 @@
 
 def main_kernel(
     ones_all, twos_all, base, s0, v0, speeds, x_odd, x_even, y_even, y_odd,
-    v1, coefs, ones_grad_high, ones_grad_low, x_even_out, x_odd_out, y_even_out, y_odd_out, sums,
+    v1, coefs, ones_grad_high, ones_grad_low, x_even_out, x_odd_out, y_odd_out, sums,
     moment_ends, cot_ends, v1_held, total, x_got, y_got, x_ends, y_ends, weights,
 ):
     w_in, b_in, w_mid, b_mid, w_out, _ = unbundled(s0, weights)
@@ -321,15 +321,19 @@
     y_ends[1] = ends[8:16]
     x_even_out[...] = x_ends[odd_x]
     x_odd_out[...] = x_ends[1 - odd_x]
-    y_even_out[...] = y_ends[odd_y]
-    y_odd_out[...] = y_ends[1 - odd_y]
+    ends = y_ends[1 - odd_y]
+    y_odd_out[0:8, :] = ends[:, 0:128]
+    y_odd_out[8:16, :] = ends[:, 128:256]
+    ends = y_ends[odd_y]
+    sums[64:72, :] = ends[:, 0:128]
+    sums[72:80, :] = ends[:, 128:256]
     first = total[:, 0:128]
     second = total[:, 128:256]
     turn = lambda item: pltpu.roll(item, 64, 1)
     rest = jnp.concatenate(
         [first[0:16], turn(second[80:96]), first[96:104], turn(first[96:104]), second[80:96]], 0
     )
-    sums[...] = jnp.where(iota((64, 128), 1) < 64, first[16:80], rest)
+    sums[0:64, :] = jnp.where(iota((64, 128), 1) < 64, first[16:80], rest)
 
 
 def tail_kernel(v1, coefs, grad_high, grad_low, s0, part, weights):
@@ -354,8 +358,11 @@
     odd_x, odd_y = parities()
     x_got[1 - odd_x] = x_even[...]
     x_got[odd_x] = x_odd[...]
-    y_got[1 - odd_y] = y_even[...]
-    y_got[odd_y] = y_odd[...]
+    at_end = jnp.logical_and(lax.axis_index("x") == 3, odd_y == 1)
+    for half in (0, 1):
+        rows, lanes = slice(64 + half * 8, 72 + half * 8), slice(half * 128, half * 128 + 128)
+        y_got[1 - odd_y, :, lanes] = y_even[rows, :]
+        y_got[odd_y, :, lanes] = jnp.where(at_end, 0.0, y_odd[rows, :])
     x_prev, x_next, y_prev, y_next = x_got.at[0], x_got.at[1], y_got.at[0], y_got.at[1]
     pick = edge_picker(8, 1024)
     ends = jnp.concatenate([y_next[...], y_prev[...]], 0).astype(bf16)
@@ -454,13 +461,13 @@
             cost_estimate=cost(5000000000, 16000000),
             name="forward",
         )(s0)
-        v1, coefs, grad_high, grad_low, x_even, x_odd, y_even, y_odd, sums = pl.pallas_call(
+        v1, coefs, grad_high, grad_low, x_even, x_odd, y_odd, sums = pl.pallas_call(
             main_kernel,
             out_shape=(
                 shape((256, 1024), f32), shape((9 * 128, 128), f32),
                 shape((64, 16384), bf16), shape((64, 16384), bf16),
                 shape((256, 128), bf16), shape((256, 128), bf16),
-                shape((8, 256), f32), shape((8, 256), f32), shape((64, 128), f32),
+                shape((16, 128), f32), shape((80, 128), f32),
             ),
             scratch_shapes=[
                 pltpu.VMEM((256, 1024), f32),
@@ -475,22 +482,22 @@
         )(
             ones_all, twos_all, base, s0, v0, speeds, x_odd, x_even, y_even, y_odd
         )
+        y_even = pairs(sums, "c", [(0, 1)])
+        sums = sums[0:64] + y_even[0:64]
+        y_odd = pairs(jnp.concatenate([sums, y_odd], 0), gy, [(1, 2), (3, 4), (5, 6), (7, 0)])
+        sums = sums + y_odd[0:64]
         steps = (
-            ("c", [(0, 1)]),
-            ("x", [(0, 1), (2, 3)]),
-            ("x", [(0, 3), (1, 2)]),
+            (gy, [(0, 4), (1, 5), (2, 6), (3, 7)]),
             ("y", [(0, 1), (2, 3)]),
             ("y", [(0, 3), (1, 2)]),
             (ring, [(0, 1), (2, 3), (4, 5), (6, 7)]),
             (ring, [(1, 2), (3, 4), (5, 6), (7, 0)]),
         )
         places = {
-            "y_odd": (gy, y_odd, [(1, 2), (3, 4), (5, 6)]),
-            "y_even": (gy, y_even, [(0, 1), (2, 3), (4, 5), (6, 7)]),
             "x_even": (gx, x_even, [(i, i + 1) for i in range(0, 15, 2)]),
             "x_odd": (gx, x_odd, [(i, i + 1) for i in range(1, 15, 2)]),
         }
-        beside = {1: ("y_odd",), 2: ("y_even",), 3: ("x_even",), 4: ("x_odd",)}
+        beside = {0: ("x_even",), 2: ("x_odd",)}
         got = {}
         for index, (axis, links) in enumerate(steps):
             moving = {}
@@ -516,7 +523,7 @@
                 *values, sums = lax.optimization_barrier(tuple(moving[n] for n in names) + (sums,))
                 got.update(zip(names, values))
         other = pairs(sums, ring, [(0, 3), (1, 6), (2, 5), (4, 7)])
-        x_even, x_odd, y_even, y_odd = (got[n] for n in ("x_even", "x_odd", "y_even", "y_odd"))
+        x_even, x_odd = got["x_even"], got["x_odd"]
         out = pl.pallas_call(
             finish_kernel,
             out_shape=shape((2048, 128), f32),

time: 79.4 us -> 78.7 us (level)
  starting transfers between devices: 29.7 us -> 27.6 us
  waiting for transfers between devices: 19.7 us -> 20.5 us
    ppermute x16 -> x14, starting transfers between devices: 29.7 us -> 27.6 us  [pairs(): lax.ppermute(value, axis, [(a, b) for a, b in links] + [(b, a) for a, b i...]
    ppermute x16 -> x14, waiting for transfers between devices: 19.7 us -> 20.5 us  [pairs(): lax.ppermute(value, axis, [(a, b) for a, b in links] + [(b, a) for a, b i...]
  transfers between devices with their start and end apart: 16 -> 14, of which waited for: 9 -> 8; matrix products, arithmetic and copies ran while one was open for 0% -> 0% of each run, Pallas kernels for 9% -> 9%
where the time goes in v3:
time: 78.7 us; the launch traced here: 77.3 us
  starting transfers between devices  27.6 us (35%)
  Pallas kernels  27.3 us (35%)
  waiting for transfers between devices  20.5 us (26%)
  local copies, waits for them, and re-layouts  1.08 us (1%)
    ppermute x14, starting transfers between devices, pairs(): lax.ppermute(value, axis, [(a, b) for a, b in links] + [(b, a) for a, b i...  27.6 us
    ppermute x14, waiting for transfers between devices, pairs(): lax.ppermute(value, axis, [(a, b) for a, b in links] + [(b, a) for a, b i...  20.5 us
    pallas_call x1, Pallas kernels, local(): pl.pallas_call(main_kernel, out_shape=(shape((256, 1024), f32), shape((9...  15 us
    pallas_call x1, Pallas kernels, local(): pl.pallas_call(pack_kernel, in_specs=[far] * 12, out_shape=(shape((304, 1...  4.35 us
    pallas_call x1, Pallas kernels, local(): pl.pallas_call(forward_kernel, out_shape=(shape((64, 16384), f32), shape(...  3.47 us
    pallas_call x1, Pallas kernels, local(): pl.pallas_call(finish_kernel, out_shape=shape((2048, 128), f32), scratch_...  2.33 us
  transfers between devices with their start and end apart: 14, of which 8 were waited for; matrix products, arithmetic and copies ran while one was open for 0% of the time, Pallas kernels for 9%

profile of v3, /device:TPU:30, one launch (start us, length us, event | category | flops | bytes accessed | tf_op | source)
XLA Modules:
  0.0 77.3 jit_solution(17885677386222338248)
XLA Ops:
  0.6 4.3 %pack.1 = (bf16[304,1024]{1,0:T(8,128)(2,1)}, f32[256,1024]{1,0:T(8,128)}, f32[512,128]{1,0:T(8,128)}, bf16[544,128]{1,0:T(8,128)(2,1)}, bf16[544,128]{1,0:T(8,1...) custom-call(f32[2048,128]{1,0:T(8,128)} %bitcast.15, bf16[2048,128]{1,0:T(8,128)(2,1)} %bitcast.17, ...), custom_call_target="tpu_custom_call" | custom-call | tf_op jit(solution)/shard_map/pack/pallas_call | solution.py:434
  5.0 4.8 %collective-permute-start = (bf16[544,128]{1,0:T(8,128)(2,1)}, bf16[544,128]{1,0:T(8,128)(2,1)S(1)}, u32[]{:S(2)}, u32[]{:S(2)}) collective-permute-start(bf16[544,128]{1,0:T(8,128)(2,1)} %get-tuple-element.49), channel_id=1, source_target_pairs={{16,32},{48,64},{80,96},{112,128},{144,160},{176,192},{208,224},{3... | collective-permute-start | bytes 417800 | tf_op jit(solution)/shard_map/ppermute | solution.py:402
  9.8 0.1 collective-permute-start.1
  9.9 0.1 collective-permute-start.2
  10.0 2.8 %collective-permute-start.3 = (f32[48,768]{1,0:T(8,128)}, f32[48,768]{1,0:T(8,128)S(1)}, u32[]{:S(2)}, u32[]{:S(2)}) collective-permute-start(f32[48,768]{1,0:T(8,128)} %get-tuple-element.52), channel_id=1, source_target_pairs={{2,4},{6,8},{10,12},{4,2},{8,6},{12,10},{3,5},{7,9},{11,13},{5,3},... | collective-permute-start | bytes 442376 | tf_op jit(solution)/shard_map/ppermute | solution.py:402
  12.9 0.0 copy-start
  12.9 1.1 %copy-done = bf16[304,1024]{1,0:T(8,128)(2,1)S(1)} copy-done((bf16[304,1024]{1,0:T(8,128)(2,1)S(1)}, bf16[304,1024]{1,0:T(8,128)(2,1)}, u32[]{:S(2)}) %copy-start) | copy-done | bytes 622616
  13.9 0.0 copy-start.1
  14.0 0.0 copy-start.2
  14.0 0.0 copy-start.3
  14.0 3.5 %forward.1 = (f32[64,16384]{1,0:T(8,128)S(1)}, f32[64,16384]{1,0:T(8,128)S(1)}, f32[256,1024]{1,0:T(8,128)S(1)}) custom-call(bf16[304,1024]{1,0:T(8,128)(2,1)S(1)} %copy-done), custom_call_target="tpu_custom_call" | custom-call | flops 5000000000 | bytes 16000000 | tf_op jit(solution)/shard_map/forward/pallas_call | solution.py:456
  17.4 1.1 %collective-permute-done.x_odd = bf16[544,128]{1,0:T(8,128)(2,1)S(1)} collective-permute-done((bf16[544,128]{1,0:T(8,128)(2,1)}, bf16[544,128]{1,0:T(8,128)(2,1)S(1)}, u32[]{:S(2)}, u32[]{:S(2)}) %collective-permute-start) | collective-permute-done | bytes 139296 | tf_op jit(solution)/shard_map/ppermute | solution.py:402
  18.5 0.0 collective-permute-done.1.x_even
  18.5 0.0 collective-permute-done.2.y_even
  18.5 0.0 collective-permute-done.3.y_odd
  18.5 0.0 copy-done.1
  18.5 0.0 copy-done.2
  18.5 0.0 copy-done.3
  18.5 15.0 %network.1 = (f32[256,1024]{1,0:T(8,128)S(1)}, f32[1152,128]{1,0:T(8,128)S(1)}, bf16[64,16384]{1,0:T(8,128)(2,1)S(1)}, bf16[64,16384]{1,0:T(8,128)(2,1)S(1)}, bf...) custom-call(f32[64,16384]{1,0:T(8,128)S(1)} %get-tuple-element.44.ones, ...), custom_call_target="tpu_custom_call" | custom-call | flops 15000000512 | bytes 40000000 | tf_op jit(solution)/shard_map/network/pallas_call | solution.py:464
  33.6 0.0 collective-permute-start.4
  33.6 1.2 %collective-permute-done.4.y_even = f32[80,128]{1,0:T(8,128)S(1)} collective-permute-done((f32[80,128]{1,0:T(8,128)S(1)}, f32[80,128]{1,0:T(8,128)S(1)}, u32[]{:S(2)}, u32[]{:S(2)}) %collective-permute-start.4) | collective-permute-done | bytes 40992 | tf_op jit(solution)/shard_map/ppermute | solution.py:402
  34.9 0.7 collective-permute-start.5
  35.5 2.8 %collective-permute-done.5.y_odd = f32[80,128]{1,0:T(8,128)S(1)} collective-permute-done((f32[80,128]{1,0:T(8,128)S(1)}, f32[80,128]{1,0:T(8,128)S(1)}, u32[]{:S(2)}, u32[]{:S(2)}) %collective-permute-start.5) | collective-permute-done | bytes 40992 | tf_op jit(solution)/shard_map/ppermute | solution.py:402
  38.4 0.9 %collective-permute-start.6 = (bf16[256,128]{1,0:T(8,128)(2,1)S(1)}, bf16[256,128]{1,0:T(8,128)(2,1)S(1)}, u32[]{:S(2)}, u32[]{:S(2)}) collective-permute-start(bf16[256,128]{1,0:T(8,128)(2,1)S(1)} %get-tuple-element.58), channel_id=1, source_target_pairs={{0,16},{32,48},{64,80},{96,112},{128,144},{160,176},{192,208},{224... | collective-permute-start | bytes 196616 | tf_op jit(solution)/shard_map/ppermute | solution.py:402
  39.2 1.7 %collective-permute-start.7 = (f32[64,128]{1,0:T(8,128)S(1)}, f32[64,128]{1,0:T(8,128)S(1)}, u32[]{:S(2)}, u32[]{:S(2)}) collective-permute-start(f32[64,128]{1,0:T(8,128)S(1)} %slice_add_fusion), channel_id=1, source_target_pairs={{0,8},{2,10},{4,12},{6,14},{8,0},{10,2},{12,4},{14,6},{1,9},{3,11}... | collective-permute-start | bytes 98312 | tf_op jit(solution)/shard_map/ppermute | solution.py:402
  41.0 3.9 %collective-permute-done.7 = f32[64,128]{1,0:T(8,128)S(1)} collective-permute-done((f32[64,128]{1,0:T(8,128)S(1)}, f32[64,128]{1,0:T(8,128)S(1)}, u32[]{:S(2)}, u32[]{:S(2)}) %collective-permute-start.7) | collective-permute-done | bytes 32800 | tf_op jit(solution)/shard_map/ppermute | solution.py:402
  44.9 0.0 collective-permute-done.6.x_even
  44.9 1.3 %collective-permute-start.8 = (f32[64,128]{1,0:T(8,128)S(1)}, f32[64,128]{1,0:T(8,128)S(1)}, u32[]{:S(2)}, u32[]{:S(2)}) collective-permute-start(f32[64,128]{1,0:T(8,128)S(1)} %add.23), channel_id=1, source_target_pairs={{0,16},{32,48},{16,0},{48,32},{1,17},{33,49},{17,1},{49,33},{2,18}... | collective-permute-start | bytes 98312 | tf_op jit(solution)/shard_map/ppermute | solution.py:402
  46.1 2.7 %collective-permute-done.8 = f32[64,128]{1,0:T(8,128)S(1)} collective-permute-done((f32[64,128]{1,0:T(8,128)S(1)}, f32[64,128]{1,0:T(8,128)S(1)}, u32[]{:S(2)}, u32[]{:S(2)}) %collective-permute-start.8) | collective-permute-done | bytes 32800 | tf_op jit(solution)/shard_map/ppermute | solution.py:402
  48.9 4.0 %collective-permute-start.9 = (bf16[256,128]{1,0:T(8,128)(2,1)S(1)}, bf16[256,128]{1,0:T(8,128)(2,1)S(1)}, u32[]{:S(2)}, u32[]{:S(2)}) collective-permute-start(bf16[256,128]{1,0:T(8,128)(2,1)S(1)} %get-tuple-element.61), channel_id=1, source_target_pairs={{16,32},{48,64},{80,96},{112,128},{144,160},{176,192},{208,224},{3... | collective-permute-start | bytes 196616 | tf_op jit(solution)/shard_map/ppermute | solution.py:402
  52.9 0.1 collective-permute-start.10
  53.0 5.4 %collective-permute-done.10 = f32[64,128]{1,0:T(8,128)S(1)} collective-permute-done((f32[64,128]{1,0:T(8,128)S(1)}, f32[64,128]{1,0:T(8,128)S(1)}, u32[]{:S(2)}, u32[]{:S(2)}) %collective-permute-start.10) | collective-permute-done | bytes 32800 | tf_op jit(solution)/shard_map/ppermute | solution.py:402
  58.5 0.0 collective-permute-done.9.x_odd
  58.5 2.0 %collective-permute-start.11 = (f32[64,128]{1,0:T(8,128)S(1)}, f32[64,128]{1,0:T(8,128)S(1)}, u32[]{:S(2)}, u32[]{:S(2)}) collective-permute-start(f32[64,128]{1,0:T(8,128)S(1)} %add.25), channel_id=1, source_target_pairs={{0,1},{64,65},{128,129},{192,193},{1,0},{65,64},{129,128},{193,192... | collective-permute-start | bytes 98312 | tf_op jit(solution)/shard_map/ppermute | solution.py:402
  60.4 1.5 %tail.1.part = f32[256,1024]{1,0:T(8,128)S(1)} custom-call(f32[256,1024]{1,0:T(8,128)S(1)} %get-tuple-element.64.v1, f32[1152,128]{1,0:T(8,128)S(1)} %get-tuple-element.65.coefs, bf16[64,16384]{1,0:T(8,128)(2,1)S(1)} %get-tuple-element.66.grad_high, bf16[64,16384]{1,0:T(8,128)(2,1)S(1)} %get-tuple-element.67.grad_low, bf16[304,1024]{1,0:T(8,128)(2,1)S(1)} %copy-done.1), custom_call_target="tpu_custom_call" | custom-call | flops 2000000000 | bytes 8000000 | tf_op jit(solution)/shard_map/tail/pallas_call | solution.py:510
  61.9 0.6 collective-permute-done.11
  62.5 2.5 %collective-permute-start.12 = (f32[64,128]{1,0:T(8,128)S(1)}, f32[64,128]{1,0:T(8,128)S(1)}, u32[]{:S(2)}, u32[]{:S(2)}) collective-permute-start(f32[64,128]{1,0:T(8,128)S(1)} %add.26), channel_id=1, source_target_pairs={{1,64},{65,128},{129,192},{193,0},{64,1},{128,65},{192,129},{0,193... | collective-permute-start | bytes 98312 | tf_op jit(solution)/shard_map/ppermute | solution.py:402
  65.0 2.6 %collective-permute-done.12 = f32[64,128]{1,0:T(8,128)S(1)} collective-permute-done((f32[64,128]{1,0:T(8,128)S(1)}, f32[64,128]{1,0:T(8,128)S(1)}, u32[]{:S(2)}, u32[]{:S(2)}) %collective-permute-start.12) | collective-permute-done | bytes 32800 | tf_op jit(solution)/shard_map/ppermute | solution.py:402
  67.6 6.7 %collective-permute-start.13 = (f32[64,128]{1,0:T(8,128)S(1)}, f32[64,128]{1,0:T(8,128)S(1)}, u32[]{:S(2)}, u32[]{:S(2)}) collective-permute-start(f32[64,128]{1,0:T(8,128)S(1)} %add.27.refs_0_), channel_id=1, source_target_pairs={{0,65},{1,192},{64,129},{128,193},{65,0},{192,1},{129,64},{193,128... | collective-permute-start | bytes 98312 | tf_op jit(solution)/shard_map/ppermute | solution.py:402
  74.3 2.3 %finish.1 = f32[2048,128]{1,0:T(8,128)} custom-call(f32[256,1024]{1,0:T(8,128)S(1)} %tail.1.part, f32[1152,128]{1,0:T(8,128)S(1)} %get-tuple-element.65.coefs, bf16[256,128]{1,0:T(8,128)(2,1)S(1)} %collective-permute-done.6.x_even, bf16[256,128]{1,0:T(8,128)(2,1)S(1)} %collective-permute-done.9.x_odd, f32[80,128]{1,0:T(8,128)S(1)} %collective-permute-done.4.y_even, ...), custom_call_target="tpu_custom_call" | custom-call | flops 10000000 | bytes 6000000 | tf_op jit(solution)/shard_map/finish/pallas_call | solution.py:527
  76.6 0.0 collective-permute-done.13.refs_1_
  76.6 0.7 weights.1
  (8 shorter events, 0.0 us)
Async XLA Ops:
  5.0 13.5 %collective-permute-start = (bf16[544,128]{1,0:T(8,128)(2,1)}, bf16[544,128]{1,0:T(8,128)(2,1)S(1)}, u32[]{:S(2)}, u32[]{:S(2)}) collective-permute-start(bf16[544,128]{1,0:T(8,128)(2,1)} %get-tuple-element.49), channel_id=1, source_target_pairs={{16,32},{48,64},{80,96},{112,128},{144,160},{176,192},{208,224},{3... | collective-permute-start | bytes 417800 | tf_op jit(solution)/shard_map/ppermute | solution.py:402
  9.8 8.7 %collective-permute-start.1 = (bf16[544,128]{1,0:T(8,128)(2,1)}, bf16[544,128]{1,0:T(8,128)(2,1)S(1)}, u32[]{:S(2)}, u32[]{:S(2)}) collective-permute-start(bf16[544,128]{1,0:T(8,128)(2,1)} %get-tuple-element.50), channel_id=1, source_target_pairs={{0,16},{32,48},{64,80},{96,112},{128,144},{160,176},{192,208},{224... | collective-permute-start | bytes 417800 | tf_op jit(solution)/shard_map/ppermute | solution.py:402
  9.9 8.6 %collective-permute-start.2 = (f32[48,768]{1,0:T(8,128)}, f32[48,768]{1,0:T(8,128)S(1)}, u32[]{:S(2)}, u32[]{:S(2)}) collective-permute-start(f32[48,768]{1,0:T(8,128)} %get-tuple-element.51), channel_id=1, source_target_pairs={{0,2},{4,6},{8,10},{12,14},{2,0},{6,4},{10,8},{14,12},{1,3},{5,7},... | collective-permute-start | bytes 442376 | tf_op jit(solution)/shard_map/ppermute | solution.py:402
  10.0 8.5 %collective-permute-start.3 = (f32[48,768]{1,0:T(8,128)}, f32[48,768]{1,0:T(8,128)S(1)}, u32[]{:S(2)}, u32[]{:S(2)}) collective-permute-start(f32[48,768]{1,0:T(8,128)} %get-tuple-element.52), channel_id=1, source_target_pairs={{2,4},{6,8},{10,12},{4,2},{8,6},{12,10},{3,5},{7,9},{11,13},{5,3},... | collective-permute-start | bytes 442376 | tf_op jit(solution)/shard_map/ppermute | solution.py:402
  12.9 1.1 %copy-start = (bf16[304,1024]{1,0:T(8,128)(2,1)S(1)}, bf16[304,1024]{1,0:T(8,128)(2,1)}, u32[]{:S(2)}) copy-start(bf16[304,1024]{1,0:T(8,128)(2,1)} %get-tuple-element.43.s0) | copy-start | bytes 1867780
  13.9 4.6 %copy-start.1 = (bf16[304,1024]{1,0:T(8,128)(2,1)S(1)}, bf16[304,1024]{1,0:T(8,128)(2,1)}, u32[]{:S(2)}) copy-start(bf16[304,1024]{1,0:T(8,128)(2,1)} %get-tuple-element.43.s0) | copy-start | bytes 1867780
  14.0 4.6 %copy-start.2 = (f32[256,1024]{1,0:T(8,128)S(1)}, f32[256,1024]{1,0:T(8,128)}, u32[]{:S(2)}) copy-start(f32[256,1024]{1,0:T(8,128)} %get-tuple-element.47.v0) | copy-start | bytes 3145732
  14.0 4.6 %copy-start.3 = (f32[512,128]{1,0:T(8,128)S(1)}, f32[512,128]{1,0:T(8,128)}, u32[]{:S(2)}) copy-start(f32[512,128]{1,0:T(8,128)} %get-tuple-element.48.speeds) | copy-start | bytes 786436
  33.6 1.3 %collective-permute-start.4 = (f32[80,128]{1,0:T(8,128)S(1)}, f32[80,128]{1,0:T(8,128)S(1)}, u32[]{:S(2)}, u32[]{:S(2)}) collective-permute-start(f32[80,128]{1,0:T(8,128)S(1)} %get-tuple-element.56), channel_id=1, source_target_pairs={{0,2},{2,0},{1,3},{3,1},{4,6},{6,4},{5,7},{7,5},{8,10},{10,8},{9,1... | collective-permute-start | bytes 122888 | tf_op jit(solution)/shard_map/ppermute | solution.py:402
  34.9 3.5 %collective-permute-start.5 = (f32[80,128]{1,0:T(8,128)S(1)}, f32[80,128]{1,0:T(8,128)S(1)}, u32[]{:S(2)}, u32[]{:S(2)}) collective-permute-start(f32[80,128]{1,0:T(8,128)S(1)} %pad_maximum_fusion), channel_id=1, source_target_pairs={{2,4},{6,8},{10,12},{14,0},{4,2},{8,6},{12,10},{0,14},{3,5},{7,9},... | collective-permute-start | bytes 122888 | tf_op jit(solution)/shard_map/ppermute | solution.py:402
  38.4 6.5 %collective-permute-start.6 = (bf16[256,128]{1,0:T(8,128)(2,1)S(1)}, bf16[256,128]{1,0:T(8,128)(2,1)S(1)}, u32[]{:S(2)}, u32[]{:S(2)}) collective-permute-start(bf16[256,128]{1,0:T(8,128)(2,1)S(1)} %get-tuple-element.58), channel_id=1, source_target_pairs={{0,16},{32,48},{64,80},{96,112},{128,144},{160,176},{192,208},{224... | collective-permute-start | bytes 196616 | tf_op jit(solution)/shard_map/ppermute | solution.py:402
  39.2 5.6 %collective-permute-start.7 = (f32[64,128]{1,0:T(8,128)S(1)}, f32[64,128]{1,0:T(8,128)S(1)}, u32[]{:S(2)}, u32[]{:S(2)}) collective-permute-start(f32[64,128]{1,0:T(8,128)S(1)} %slice_add_fusion), channel_id=1, source_target_pairs={{0,8},{2,10},{4,12},{6,14},{8,0},{10,2},{12,4},{14,6},{1,9},{3,11}... | collective-permute-start | bytes 98312 | tf_op jit(solution)/shard_map/ppermute | solution.py:402
  44.9 4.0 %collective-permute-start.8 = (f32[64,128]{1,0:T(8,128)S(1)}, f32[64,128]{1,0:T(8,128)S(1)}, u32[]{:S(2)}, u32[]{:S(2)}) collective-permute-start(f32[64,128]{1,0:T(8,128)S(1)} %add.23), channel_id=1, source_target_pairs={{0,16},{32,48},{16,0},{48,32},{1,17},{33,49},{17,1},{49,33},{2,18}... | collective-permute-start | bytes 98312 | tf_op jit(solution)/shard_map/ppermute | solution.py:402
  48.9 9.6 %collective-permute-start.9 = (bf16[256,128]{1,0:T(8,128)(2,1)S(1)}, bf16[256,128]{1,0:T(8,128)(2,1)S(1)}, u32[]{:S(2)}, u32[]{:S(2)}) collective-permute-start(bf16[256,128]{1,0:T(8,128)(2,1)S(1)} %get-tuple-element.61), channel_id=1, source_target_pairs={{16,32},{48,64},{80,96},{112,128},{144,160},{176,192},{208,224},{3... | collective-permute-start | bytes 196616 | tf_op jit(solution)/shard_map/ppermute | solution.py:402
  52.9 5.5 %collective-permute-start.10 = (f32[64,128]{1,0:T(8,128)S(1)}, f32[64,128]{1,0:T(8,128)S(1)}, u32[]{:S(2)}, u32[]{:S(2)}) collective-permute-start(f32[64,128]{1,0:T(8,128)S(1)} %add.24), channel_id=1, source_target_pairs={{0,48},{16,32},{48,0},{32,16},{1,49},{17,33},{49,1},{33,17},{2,50}... | collective-permute-start | bytes 98312 | tf_op jit(solution)/shard_map/ppermute | solution.py:402
  58.5 4.0 %collective-permute-start.11 = (f32[64,128]{1,0:T(8,128)S(1)}, f32[64,128]{1,0:T(8,128)S(1)}, u32[]{:S(2)}, u32[]{:S(2)}) collective-permute-start(f32[64,128]{1,0:T(8,128)S(1)} %add.25), channel_id=1, source_target_pairs={{0,1},{64,65},{128,129},{192,193},{1,0},{65,64},{129,128},{193,192... | collective-permute-start | bytes 98312 | tf_op jit(solution)/shard_map/ppermute | solution.py:402
  62.5 5.1 %collective-permute-start.12 = (f32[64,128]{1,0:T(8,128)S(1)}, f32[64,128]{1,0:T(8,128)S(1)}, u32[]{:S(2)}, u32[]{:S(2)}) collective-permute-start(f32[64,128]{1,0:T(8,128)S(1)} %add.26), channel_id=1, source_target_pairs={{1,64},{65,128},{129,192},{193,0},{64,1},{128,65},{192,129},{0,193... | collective-permute-start | bytes 98312 | tf_op jit(solution)/shard_map/ppermute | solution.py:402
  67.6 9.0 %collective-permute-start.13 = (f32[64,128]{1,0:T(8,128)S(1)}, f32[64,128]{1,0:T(8,128)S(1)}, u32[]{:S(2)}, u32[]{:S(2)}) collective-permute-start(f32[64,128]{1,0:T(8,128)S(1)} %add.27.refs_0_), channel_id=1, source_target_pairs={{0,65},{1,192},{64,129},{128,193},{65,0},{192,1},{129,64},{193,128... | collective-permute-start | bytes 98312 | tf_op jit(solution)/shard_map/ppermute | solution.py:402
